TPU v7x, 512 devices: a whole 4x8x8 slice. The times are simulated.
512 devices in a mesh: slab: 128 (over y, z, core), grp: 4 (over x).
Axes of the slice: x: 4, y: 8, z: 8, core: 2. Of those that a mesh axis runs over, the one named last changes fastest.
Arguments:
- potential: bfloat16 [1024, 8, 1024], P('slab'), may hold values from -3 to 3
- coefficients: bfloat16 [2048, 16, 8, 1024], P(('slab', 'grp')), may hold values from -1 to 1
- box_center: int32 [2048], replicated, may hold values from 0 to 1023, as said below
- box_extent: int32 [2048], replicated, may hold values from 8 to 16
Outputs:
- margin: float32 [2048, 80], P(('slab', 'grp'))
- hamiltonian: float32 [2048, 80], P(('slab', 'grp'))
Inputs may be any that keep to these rules, and one draw needn't show every extreme that they name: `box_center`: function b's centre lies among the 8 planes of slab b // 16, that is from (8 * (b // 16)) on.
All inputs are finite; a program needn't handle non-finite values.
Results may differ from a plain program's by a relative error of at most 0.0003.
Values may be sent and summed in bfloat16 or wider, within the bound.
No kernel may reach another device: no remote copies, remote signals or barrier semaphores. Data moves between devices by JAX's collectives and lax.ppermute only.
A program may use at most 64 MiB of HBM per device.

v0:
```python
import jax
import jax.numpy as jnp
from jax import lax
from jax.sharding import PartitionSpec as P

COMP = 8
CX = 32
CY = 32


def with_halo(value, sides, width):
    for axis, dim in sides:
        size, length = (lax.axis_size(axis), value.shape[dim])
        up = [(i, (i + 1) % size) for i in range(size)]
        down = [(j, i) for i, j in up]
        last = lax.slice_in_dim(value, length - width, length, axis=dim)
        initial = lax.slice_in_dim(value, 0, width, axis=dim)
        before = lax.ppermute(last, axis, up)
        after = lax.ppermute(initial, axis, down)
        value = jnp.concatenate([before, value, after], axis=dim)
    return value


def in_one_piece(arrays, axis, split_dim, concat_dim, along):
    both = jnp.concatenate(arrays, axis=along)
    filled, at, done = (
        lax.all_to_all(both, axis, split_axis=split_dim, concat_axis=concat_dim, tiled=True),
        0,
        [],
    )
    for a in arrays:
        done.append(lax.slice_in_dim(filled, at, at + a.shape[along], axis=along))
        at += a.shape[along]
    return tuple(done)


def shifted(value, axis, steps):
    count = lax.axis_size(axis)
    pairs = [(source, (source + steps) % count) for source in range(count)]
    return lax.ppermute(value, axis, pairs)


def split_up(value, dim, size):
    lengths = value.shape
    blocks = value.reshape(*lengths[:dim], size, lengths[dim] // size, *lengths[dim + 1 :])
    return jnp.moveaxis(blocks, dim, 0)


def sent_and_summed(value, axis, dim):
    size = lax.axis_size(axis)
    blocks = lax.all_to_all(split_up(value, dim, size), axis, 0, 0, tiled=True)
    return jnp.sum(blocks, axis=0)


def sent_together(arrays, axis, dim, along):
    ends, at = ([], 0)
    for a in arrays[:-1]:
        at += a.shape[along]
        ends.append(at)
    both = jnp.concatenate(arrays, axis=along)
    return tuple(jnp.split(sent_and_summed(both, axis, dim), ends, axis=along))


def haar_signs():
    row_ids = jnp.arange(COMP, dtype=jnp.int32)[:, None]
    col_ids = jnp.arange(COMP, dtype=jnp.int32)[None, :]
    common = jnp.bitwise_and(row_ids, col_ids)
    parity = (common % 2 + common // 2 % 2 + common // 4 % 2) % 2
    return (1 - 2 * parity).astype(jnp.float32)


def laplace_plane():
    cells = jnp.arange(CX * CY, dtype=jnp.int32)
    first_x = (cells // CY)[:, None]
    second_x = (cells // CY)[None, :]
    first_y = (cells % CY)[:, None]
    second_y = (cells % CY)[None, :]
    step_x = jnp.abs(first_x - second_x)
    step_y = jnp.abs(first_y - second_y)
    beside = (step_x == 1) & (first_y == second_y) | (step_y == 1) & (first_x == second_x)
    same_cell = (first_x == second_x) & (first_y == second_y)
    return jnp.where(same_cell, 2.0, jnp.where(beside, -0.5, 0.0)).astype(jnp.bfloat16)


def apply_hamiltonian(orbital, pot_box, inside):
    cell_count = orbital.shape[3]
    plane_term = jnp.dot(
        orbital.reshape(-1, cell_count), laplace_plane(), preferred_element_type=jnp.float32
    ).reshape(orbital.shape)
    padded = jnp.pad(orbital, ((0, 0), (1, 1), (0, 0), (0, 0)))
    depth_term = orbital.astype(jnp.float32) - 0.5 * (
        padded[:, :-2].astype(jnp.float32) + padded[:, 2:].astype(jnp.float32)
    )
    haar_table = haar_signs()
    fine_values = jnp.einsum(
        "kc,npcx->npkx",
        haar_table.astype(jnp.bfloat16),
        orbital,
        preferred_element_type=jnp.float32,
    )
    potential_term = (
        jnp.einsum(
            "kc,npkx->npcx",
            haar_table,
            pot_box.astype(jnp.float32) * fine_values,
            precision=lax.Precision.HIGHEST,
        )
        / COMP
    )
    return jnp.where(inside, plane_term + depth_term + potential_term, 0.0).astype(jnp.bfloat16)


def place_planes(starts, frame_depth, tile_data):
    source = jnp.arange(tile_data.shape[1], dtype=jnp.int32)
    target = jnp.arange(frame_depth, dtype=jnp.int32)
    onehot = (starts[:, None, None] + source[None, None, :] == target[None, :, None]).astype(
        jnp.bfloat16
    )
    placed = jnp.einsum("nqp,npcx->nqcx", onehot, tile_data, preferred_element_type=jnp.float32)
    return placed.astype(jnp.bfloat16)


def into_band(block_rows, offset, members):
    return jnp.pad(block_rows, ((0, 0), (offset * members, (2 - offset) * members)))


def local(potential, coefficients, box_center, box_extent):
    slab_index = lax.axis_index("slab")
    group_index = lax.axis_index("grp")
    slab_count = lax.axis_size("slab")
    groups = lax.axis_size("grp")
    per_device = coefficients.shape[0]
    box_depth = coefficients.shape[1]
    slab_depth = potential.shape[0]
    rim_depth = box_depth // 2
    members = groups * per_device
    first_row = (slab_index * groups + group_index) * per_device
    centers = lax.dynamic_slice_in_dim(box_center, first_row, per_device)
    extents = lax.dynamic_slice_in_dim(box_extent, first_row, per_device)
    frame_starts = centers - slab_index * slab_depth - extents // 2 + rim_depth
    planes = jnp.arange(box_depth, dtype=jnp.int32)
    inside = (planes[None, :] < extents[:, None])[:, :, None, None]
    orbital = jnp.where(inside, coefficients, jnp.zeros((), jnp.bfloat16))
    pot_frame = with_halo(potential, (("slab", 0),), rim_depth)
    padded_pot = jnp.pad(pot_frame, ((0, box_depth), (0, 0), (0, 0)))

    def cut_box(start_at):
        return lax.dynamic_slice_in_dim(padded_pot, start_at, box_depth, 0)

    pot_box = jax.vmap(cut_box)(frame_starts)
    applied = apply_hamiltonian(orbital, pot_box, inside)
    got_orbital, got_applied = in_one_piece((orbital, applied), "grp", 3, 0, 1)

    def region_starts(source_slab, step):
        slab_centers = lax.dynamic_slice_in_dim(box_center, source_slab * members, members)
        slab_extents = lax.dynamic_slice_in_dim(box_extent, source_slab * members, members)
        return slab_centers - source_slab * slab_depth - slab_extents // 2 + step * slab_depth

    own_starts = region_starts(slab_index, 0)
    middle_orbital = place_planes(own_starts, slab_depth, got_orbital)
    middle_applied = place_planes(own_starts, slab_depth, got_applied)
    lower_set = None
    upper_set = None
    for direction in (1, -1):
        came_orbital, came_applied = shifted((got_orbital, got_applied), "slab", direction)
        source_slab = (slab_index - direction) % slab_count
        came_starts = region_starts(source_slab, -direction)
        placed_pair = (
            place_planes(came_starts, slab_depth, came_orbital),
            place_planes(came_starts, slab_depth, came_applied),
        )
        if direction == 1:
            lower_set = placed_pair
        else:
            upper_set = placed_pair
    tile_orbital = jnp.concatenate([lower_set[0], middle_orbital, upper_set[0]], axis=0)
    tile_applied = jnp.concatenate([lower_set[1], middle_applied, upper_set[1]], axis=0)
    flat_orbital = tile_orbital.reshape(tile_orbital.shape[0], -1)
    flat_applied = tile_applied.reshape(tile_applied.shape[0], -1)
    contract = (((1,), (1,)), ((), ()))
    part_margin = lax.dot_general(
        flat_orbital, flat_orbital, contract, preferred_element_type=jnp.float32
    )
    part_ham = lax.dot_general(
        flat_applied, flat_orbital, contract, preferred_element_type=jnp.float32
    )
    total_margin = into_band(part_margin[members : 2 * members], 1, members)
    total_ham = into_band(part_ham[members : 2 * members], 1, members)
    for direction in (1, -1):
        if direction == 1:
            sent_margin = part_margin[2 * members :]
            sent_ham = part_ham[2 * members :]
        else:
            sent_margin = part_margin[:members]
            sent_ham = part_ham[:members]
        came_margin, came_ham = shifted((sent_margin, sent_ham), "slab", direction)
        offset = 0 if direction == 1 else 2
        total_margin = total_margin + into_band(came_margin, offset, members)
        total_ham = total_ham + into_band(came_ham, offset, members)
    margin, hamiltonian = sent_together((total_margin, total_ham), "grp", 0, 1)
    return (margin, hamiltonian)


def solution(mesh):
    return jax.shard_map(
        local,
        mesh=mesh,
        in_specs=(P("slab", None, None), P(("slab", "grp"), None, None, None), P(), P()),
        out_specs=(P(("slab", "grp"), None), P(("slab", "grp"), None)),
        check_vma=False,
    )
```

profile of v0, /device:TPU:2, one launch (start us, length us, event | category | flops | bytes accessed | tf_op | source)
XLA Modules:
  0.0 153.1 jit_solution(7321663072828297707)
XLA Ops:
  0.6 1.9 %collective-permute-start = (bf16[8,8,1024]{2,1,0:T(8,128)(2,1)}, bf16[8,8,1024]{2,1,0:T(8,128)(2,1)S(1)}, u32[]{:S(2)}, u32[]{:S(2)}) collective-permute-start(bf16[8,8,1024]{2,1,0:T(8,128)(2,1)} %param.4), channel_id=1, source_target_pairs={{0,4},{4,8},{8,12},{12,16},{16,20},{20,24},{24,28},{28,32},{32,36}... | collective-permute-start | bytes 393224 | tf_op jit(solution)/shard_map/ppermute | solution.py:18
  2.6 13.3 %collective-permute-start.1 = (bf16[8,8,1024]{2,1,0:T(8,128)(2,1)}, bf16[8,8,1024]{2,1,0:T(8,128)(2,1)S(1)}, u32[]{:S(2)}, u32[]{:S(2)}) collective-permute-start(bf16[8,8,1024]{2,1,0:T(8,128)(2,1)} %param.4), channel_id=1, source_target_pairs={{4,0},{8,4},{12,8},{16,12},{20,16},{24,20},{28,24},{32,28},{36,32}... | collective-permute-start | bytes 393224 | tf_op jit(solution)/shard_map/ppermute | solution.py:19
  15.9 0.8 fusion.78
  16.8 1.4 broadcast_select_fusion
  18.1 5.2 %fusion.2 = f32[4,16,8,1024]{3,2,1,0:T(8,128)} fusion(bf16[4,16,8,1024]{3,2,1,0:T(8,128)(2,1)S(1)} %broadcast_select_fusion, s32[1024]{0:T(1024)S(1)} %get-tuple-element.17, s32[1024]{0:T(1024)S(1)} %get-tuple-element.18), kind=kOutput, calls=%fused_computation.9 | convolution fusion | flops 1089470464 | bytes 3153920 | tf_op jit(solution)/shard_map/dot_general | solution.py:87
  23.3 0.5 fusion.71
  23.8 0.3 copy-done
  24.2 0.9 fusion.33
  25.1 2.7 %gather_fusion = bf16[4,16,8,1024]{3,2,1,0:T(8,128)(2,1)} fusion(bf16[40,8,1024]{2,1,0:T(8,128)(2,1)} %fusion.33, s32[4]{0:T(128)S(1)} %get-tuple-element.2), kind=kCustom, calls=%fused_computation | custom fusion | bytes 2097200 | tf_op jit(solution)/shard_map/vmap()/gather | solution.py:148
  27.8 4.4 %fusion.5 = bf16[4,16,8,1024]{3,2,1,0:T(8,128)(2,1)S(1)} fusion(f32[4,16,8,1024]{3,2,1,0:T(8,128)} %fusion.2, bf16[4,16,8,1024]{3,2,1,0:T(8,128)(2,1)S(1)} %broadcast_select_fusion, f32[4,16,1024,8]{2,3,1,0:T(8,128)S(1)} %fusion.71, bf16[4,16,8,1024]{3,2,1,0:T(8,128)(2,1)} %gather_fusion, pred[4,16]{1,0:T(4,128)(4,1)S(1)} %iota_compare_fusion.4), kind=kOutput, calls=%fused_computation.13 | convolution fusion | flops 57151744 | bytes 7340096 | tf_op jit(solution)/shard_map/kc,npkx->npcx/dot_general | solution.py:102
  32.4 13.6 %copy.16 = bf16[4,32,8,1024]{1,2,0,3:T(8,128)(2,1)} copy(bf16[4,32,8,1024]{3,2,1,0:T(8,128)(2,1)S(1)} %pad_maximum_fusion) | data formatting | bytes 4194304 | tf_op jit(solution)/shard_map/concatenate | solution.py:25
  46.0 10.6 %reshape.161 = bf16[4,2,131072]{2,1,0:T(2,128)(2,1)} reshape(bf16[1024,4,8,32]{3,2,1,0:T(8,128)(2,1)} %bitcast.62) | data formatting | bytes 4194304
  56.5 4.8 %all-to-all-start = ((bf16[4,2,131072]{2,1,0:T(2,128)(2,1)}), bf16[4,2,131072]{2,1,0:T(2,128)(2,1)S(1)}, u32[]{:S(2)}, u32[]{:S(2)}) async-start(bf16[4,2,131072]{2,1,0:T(2,128)(2,1)} %reshape.161), calls=%async_computation | async-start | bytes 4194304 | tf_op jit(solution)/shard_map/all_to_all | solution.py:27
  61.4 19.1 %all-to-all-done = bf16[4,2,131072]{2,1,0:T(2,128)(2,1)S(1)} async-done(((bf16[4,2,131072]{2,1,0:T(2,128)(2,1)}), bf16[4,2,131072]{2,1,0:T(2,128)(2,1)S(1)}, u32[]{:S(2)}, u32[]{:S(2)}) %all-to-all-start) | async-done | bytes 2097184 | tf_op jit(solution)/shard_map/all_to_all | solution.py:27
  80.5 5.6 %reshape.162 = bf16[1024,4,8,32]{3,2,1,0:T(8,128)(2,1)} reshape(bf16[4,2,131072]{2,1,0:T(2,128)(2,1)S(1)} %all-to-all-done) | data formatting | bytes 4194304
  86.1 9.0 %copy.17 = bf16[4,32,8,4,256]{4,1,2,0,3:T(8,128)(2,1)S(1)} copy(bf16[4,32,8,4,256]{1,2,0,4,3:T(8,128)(2,1)} %bitcast.63) | data formatting | bytes 4194304 | tf_op jit(solution)/shard_map/all_to_all | solution.py:27
  95.3 1.9 %collective-permute-start.2 = (bf16[16,16,8,256]{3,1,2,0:T(8,128)(2,1)S(1)}, bf16[16,16,8,256]{3,1,2,0:T(8,128)(2,1)S(1)}, u32[]{:S(2)}, u32[]{:S(2)}) collective-permute-start(bf16[16,16,8,256]{3,1,2,0:T(8,128)(2,1)S(1)} %get-tuple-element.5), channel_id=1, source_target_pairs={{0,4},{4,8},{8,12},{12,16},{16,20},{20,24},{24,28},{28,32},{32,36}... | collective-permute-start | bytes 3145736 | tf_op jit(solution)/shard_map/ppermute | solution.py:40
  97.2 0.9 subtract_add_fusion.1
  98.1 7.0 %collective-permute-start.3 = (bf16[16,16,8,256]{3,1,2,0:T(8,128)(2,1)S(1)}, bf16[16,16,8,256]{3,1,2,0:T(8,128)(2,1)S(1)}, u32[]{:S(2)}, u32[]{:S(2)}) collective-permute-start(bf16[16,16,8,256]{3,1,2,0:T(8,128)(2,1)S(1)} %get-tuple-element.5), channel_id=1, source_target_pairs={{0,508},{4,0},{8,4},{12,8},{16,12},{20,16},{24,20},{28,24},{32,28}... | collective-permute-start | bytes 3145736 | tf_op jit(solution)/shard_map/ppermute | solution.py:40
  105.2 4.0 %collective-permute-start.7 = (bf16[16,16,8,256]{3,1,2,0:T(8,128)(2,1)S(1)}, bf16[16,16,8,256]{3,1,2,0:T(8,128)(2,1)S(1)}, u32[]{:S(2)}, u32[]{:S(2)}) collective-permute-start(bf16[16,16,8,256]{3,1,2,0:T(8,128)(2,1)S(1)} %get-tuple-element.4), channel_id=1, source_target_pairs={{0,508},{4,0},{8,4},{12,8},{16,12},{20,16},{24,20},{28,24},{32,28}... | collective-permute-start | bytes 3145736 | tf_op jit(solution)/shard_map/ppermute | solution.py:40
  109.2 1.9 %collective-permute-start.6 = (bf16[16,16,8,256]{3,1,2,0:T(8,128)(2,1)S(1)}, bf16[16,16,8,256]{3,1,2,0:T(8,128)(2,1)S(1)}, u32[]{:S(2)}, u32[]{:S(2)}) collective-permute-start(bf16[16,16,8,256]{3,1,2,0:T(8,128)(2,1)S(1)} %get-tuple-element.4), channel_id=1, source_target_pairs={{0,4},{4,8},{8,12},{12,16},{16,20},{20,24},{24,28},{28,32},{32,36}... | collective-permute-start | bytes 3145736 | tf_op jit(solution)/shard_map/ppermute | solution.py:40
  111.7 3.0 %collective-permute-done.2 = bf16[16,16,8,256]{3,1,2,0:T(8,128)(2,1)S(1)} collective-permute-done((bf16[16,16,8,256]{3,1,2,0:T(8,128)(2,1)S(1)}, bf16[16,16,8,256]{3,1,2,0:T(8,128)(2,1)S(1)}, u32[]{:S(2)}, u32[]{:S(2)}) %collective-permute-start.2) | collective-permute-done | bytes 1048608 | tf_op jit(solution)/shard_map/ppermute | solution.py:40
  115.0 2.3 %collective-permute-done.3 = bf16[16,16,8,256]{3,1,2,0:T(8,128)(2,1)S(1)} collective-permute-done((bf16[16,16,8,256]{3,1,2,0:T(8,128)(2,1)S(1)}, bf16[16,16,8,256]{3,1,2,0:T(8,128)(2,1)S(1)}, u32[]{:S(2)}, u32[]{:S(2)}) %collective-permute-start.3) | collective-permute-done | bytes 1048608 | tf_op jit(solution)/shard_map/ppermute | solution.py:40
  117.8 3.3 %fusion.24 = f32[48,48]{1,0:T(8,128)S(1)} fusion(bf16[48,8,8,256]{3,1,2,0:T(8,128)(2,1)S(1)} %pad_maximum_fusion.1), kind=kOutput, calls=%fused_computation.42 | convolution fusion | flops 75497472 | bytes 1582080 | tf_op jit(solution)/shard_map/dot_general | solution.py:181
  121.1 1.9 %collective-permute-start.4 = (f32[16,48]{1,0:T(8,128)S(1)}, f32[16,48]{1,0:T(8,128)S(1)}, u32[]{:S(2)}, u32[]{:S(2)}) collective-permute-start(f32[16,48]{1,0:T(8,128)S(1)} %get-tuple-element.8), channel_id=1, source_target_pairs={{0,4},{4,8},{8,12},{12,16},{16,20},{20,24},{24,28},{28,32},{32,36}... | collective-permute-start | bytes 9224 | tf_op jit(solution)/shard_map/ppermute | solution.py:40
  123.1 7.1 %collective-permute-start.5 = (f32[16,48]{1,0:T(8,128)S(1)}, f32[16,48]{1,0:T(8,128)S(1)}, u32[]{:S(2)}, u32[]{:S(2)}) collective-permute-start(f32[16,48]{1,0:T(8,128)S(1)} %get-tuple-element.7), channel_id=1, source_target_pairs={{0,508},{4,0},{8,4},{12,8},{16,12},{20,16},{24,20},{28,24},{32,28}... | collective-permute-start | bytes 9224 | tf_op jit(solution)/shard_map/ppermute | solution.py:40
  131.0 3.3 %fusion.27 = f32[48,48]{1,0:T(8,128)S(1)} fusion(bf16[48,8,8,256]{3,1,2,0:T(8,128)(2,1)S(1)} %pad_maximum_fusion.1, bf16[48,8,8,256]{3,1,2,0:T(8,128)(2,1)S(1)} %pad_maximum_fusion.2), kind=kOutput, calls=%fused_computation.43 | convolution fusion | flops 75497472 | bytes 3154944 | tf_op jit(solution)/shard_map/dot_general | solution.py:184
  134.3 1.9 %collective-permute-start.8 = (f32[16,48]{1,0:T(8,128)S(1)}, f32[16,48]{1,0:T(8,128)S(1)}, u32[]{:S(2)}, u32[]{:S(2)}) collective-permute-start(f32[16,48]{1,0:T(8,128)S(1)} %get-tuple-element.11), channel_id=1, source_target_pairs={{0,4},{4,8},{8,12},{12,16},{16,20},{20,24},{24,28},{28,32},{32,36}... | collective-permute-start | bytes 9224 | tf_op jit(solution)/shard_map/ppermute | solution.py:40
  136.3 7.0 %collective-permute-start.9 = (f32[16,48]{1,0:T(8,128)S(1)}, f32[16,48]{1,0:T(8,128)S(1)}, u32[]{:S(2)}, u32[]{:S(2)}) collective-permute-start(f32[16,48]{1,0:T(8,128)S(1)} %get-tuple-element.10), channel_id=1, source_target_pairs={{0,508},{4,0},{8,4},{12,8},{16,12},{20,16},{24,20},{28,24},{32,28}... | collective-permute-start | bytes 9224 | tf_op jit(solution)/shard_map/ppermute | solution.py:40
  143.3 1.2 collective-permute-done.9
  144.7 7.7 %all_to_all.23 = f32[4,4,160]{2,1,0:T(4,128)S(1)} all-to-all(f32[4,4,160]{2,1,0:T(4,128)S(1)} %reshape.140), channel_id=1, replica_groups=mesh['slab'=128,'grp'=4] {'grp'}, dimensions={0} | all-to-all | bytes 20480 | tf_op jit(solution)/shard_map/all_to_all | solution.py:51
  152.5 0.7 fusion.98
  (29 shorter events, 3.0 us)
Async XLA Ops:
  0.6 23.2 %collective-permute-start = (bf16[8,8,1024]{2,1,0:T(8,128)(2,1)}, bf16[8,8,1024]{2,1,0:T(8,128)(2,1)S(1)}, u32[]{:S(2)}, u32[]{:S(2)}) collective-permute-start(bf16[8,8,1024]{2,1,0:T(8,128)(2,1)} %param.4), channel_id=1, source_target_pairs={{0,4},{4,8},{8,12},{12,16},{16,20},{20,24},{24,28},{28,32},{32,36}... | collective-permute-start | bytes 393224 | tf_op jit(solution)/shard_map/ppermute | solution.py:18
  2.6 21.3 %collective-permute-start.1 = (bf16[8,8,1024]{2,1,0:T(8,128)(2,1)}, bf16[8,8,1024]{2,1,0:T(8,128)(2,1)S(1)}, u32[]{:S(2)}, u32[]{:S(2)}) collective-permute-start(bf16[8,8,1024]{2,1,0:T(8,128)(2,1)} %param.4), channel_id=1, source_target_pairs={{4,0},{8,4},{12,8},{16,12},{20,16},{24,20},{28,24},{32,28},{36,32}... | collective-permute-start | bytes 393224 | tf_op jit(solution)/shard_map/ppermute | solution.py:19
  23.3 0.9 copy-start
  56.5 23.9 %all-to-all-start = ((bf16[4,2,131072]{2,1,0:T(2,128)(2,1)}), bf16[4,2,131072]{2,1,0:T(2,128)(2,1)S(1)}, u32[]{:S(2)}, u32[]{:S(2)}) async-start(bf16[4,2,131072]{2,1,0:T(2,128)(2,1)} %reshape.161), calls=%async_computation | async-start | bytes 4194304 | tf_op jit(solution)/shard_map/all_to_all | solution.py:27
  95.3 19.4 %collective-permute-start.2 = (bf16[16,16,8,256]{3,1,2,0:T(8,128)(2,1)S(1)}, bf16[16,16,8,256]{3,1,2,0:T(8,128)(2,1)S(1)}, u32[]{:S(2)}, u32[]{:S(2)}) collective-permute-start(bf16[16,16,8,256]{3,1,2,0:T(8,128)(2,1)S(1)} %get-tuple-element.5), channel_id=1, source_target_pairs={{0,4},{4,8},{8,12},{12,16},{16,20},{20,24},{24,28},{28,32},{32,36}... | collective-permute-start | bytes 3145736 | tf_op jit(solution)/shard_map/ppermute | solution.py:40
  98.1 19.3 %collective-permute-start.3 = (bf16[16,16,8,256]{3,1,2,0:T(8,128)(2,1)S(1)}, bf16[16,16,8,256]{3,1,2,0:T(8,128)(2,1)S(1)}, u32[]{:S(2)}, u32[]{:S(2)}) collective-permute-start(bf16[16,16,8,256]{3,1,2,0:T(8,128)(2,1)S(1)} %get-tuple-element.5), channel_id=1, source_target_pairs={{0,508},{4,0},{8,4},{12,8},{16,12},{20,16},{24,20},{28,24},{32,28}... | collective-permute-start | bytes 3145736 | tf_op jit(solution)/shard_map/ppermute | solution.py:40
  105.2 25.0 %collective-permute-start.7 = (bf16[16,16,8,256]{3,1,2,0:T(8,128)(2,1)S(1)}, bf16[16,16,8,256]{3,1,2,0:T(8,128)(2,1)S(1)}, u32[]{:S(2)}, u32[]{:S(2)}) collective-permute-start(bf16[16,16,8,256]{3,1,2,0:T(8,128)(2,1)S(1)} %get-tuple-element.4), channel_id=1, source_target_pairs={{0,508},{4,0},{8,4},{12,8},{16,12},{20,16},{24,20},{28,24},{32,28}... | collective-permute-start | bytes 3145736 | tf_op jit(solution)/shard_map/ppermute | solution.py:40
  109.2 21.3 %collective-permute-start.6 = (bf16[16,16,8,256]{3,1,2,0:T(8,128)(2,1)S(1)}, bf16[16,16,8,256]{3,1,2,0:T(8,128)(2,1)S(1)}, u32[]{:S(2)}, u32[]{:S(2)}) collective-permute-start(bf16[16,16,8,256]{3,1,2,0:T(8,128)(2,1)S(1)} %get-tuple-element.4), channel_id=1, source_target_pairs={{0,4},{4,8},{8,12},{12,16},{16,20},{20,24},{24,28},{28,32},{32,36}... | collective-permute-start | bytes 3145736 | tf_op jit(solution)/shard_map/ppermute | solution.py:40
  121.1 22.1 %collective-permute-start.4 = (f32[16,48]{1,0:T(8,128)S(1)}, f32[16,48]{1,0:T(8,128)S(1)}, u32[]{:S(2)}, u32[]{:S(2)}) collective-permute-start(f32[16,48]{1,0:T(8,128)S(1)} %get-tuple-element.8), channel_id=1, source_target_pairs={{0,4},{4,8},{8,12},{12,16},{16,20},{20,24},{24,28},{28,32},{32,36}... | collective-permute-start | bytes 9224 | tf_op jit(solution)/shard_map/ppermute | solution.py:40
  123.1 20.2 %collective-permute-start.5 = (f32[16,48]{1,0:T(8,128)S(1)}, f32[16,48]{1,0:T(8,128)S(1)}, u32[]{:S(2)}, u32[]{:S(2)}) collective-permute-start(f32[16,48]{1,0:T(8,128)S(1)} %get-tuple-element.7), channel_id=1, source_target_pairs={{0,508},{4,0},{8,4},{12,8},{16,12},{20,16},{24,20},{28,24},{32,28}... | collective-permute-start | bytes 9224 | tf_op jit(solution)/shard_map/ppermute | solution.py:40
  134.3 9.0 %collective-permute-start.8 = (f32[16,48]{1,0:T(8,128)S(1)}, f32[16,48]{1,0:T(8,128)S(1)}, u32[]{:S(2)}, u32[]{:S(2)}) collective-permute-start(f32[16,48]{1,0:T(8,128)S(1)} %get-tuple-element.11), channel_id=1, source_target_pairs={{0,4},{4,8},{8,12},{12,16},{16,20},{20,24},{24,28},{28,32},{32,36}... | collective-permute-start | bytes 9224 | tf_op jit(solution)/shard_map/ppermute | solution.py:40
  136.3 8.3 %collective-permute-start.9 = (f32[16,48]{1,0:T(8,128)S(1)}, f32[16,48]{1,0:T(8,128)S(1)}, u32[]{:S(2)}, u32[]{:S(2)}) collective-permute-start(f32[16,48]{1,0:T(8,128)S(1)} %get-tuple-element.10), channel_id=1, source_target_pairs={{0,508},{4,0},{8,4},{12,8},{16,12},{20,16},{24,20},{28,24},{32,28}... | collective-permute-start | bytes 9224 | tf_op jit(solution)/shard_map/ppermute | solution.py:40
where the time goes:
time: 154 us; the launch traced here: 153 us
  starting transfers between devices  52.8 us (34%)
  local copies, waits for them, and re-layouts  42.6 us (28%)
  waiting for transfers between devices  25.7 us (17%)
  matrix products  18.5 us (12%)
  blocking collectives  7.7 us (5%)
  other arithmetic  4.94 us (3%)
    ppermute x8, starting transfers between devices, shifted(): return lax.ppermute(value, axis, pairs)  32.7 us
    all_to_all x1, waiting for transfers between devices, in_one_piece(): lax.all_to_all(both, axis, split_axis=split_dim, concat_axis=concat_dim,...  19.1 us
    unnamed x4, local copies, waits for them, and re-layouts  16.5 us
    concatenate x1, local copies, waits for them, and re-layouts, in_one_piece(): both = jnp.concatenate(arrays, axis=along)  13.6 us
    ppermute x1, starting transfers between devices, with_halo(): after = lax.ppermute(initial, axis, down)  13.3 us
    all_to_all x1, local copies, waits for them, and re-layouts, in_one_piece(): lax.all_to_all(both, axis, split_axis=split_dim, concat_axis=concat_dim,...  8.96 us
    all_to_all x1, blocking collectives, sent_and_summed(): blocks = lax.all_to_all(split_up(value, dim, size), axis, 0, 0, tiled=True)  7.7 us
    ppermute x8, waiting for transfers between devices, shifted(): return lax.ppermute(value, axis, pairs)  6.6 us
  transfers between devices with their start and end apart: 11, of which 4 were waited for; matrix products, arithmetic and copies ran while one was open for 12% of the time, Pallas kernels for 0%

commit v1 on v0

v1 whole, which is shorter than its diff:
```python
import jax
import jax.numpy as jnp
from jax import lax
from jax.experimental import pallas as pl
from jax.experimental.pallas import tpu as pltpu
from jax.sharding import PartitionSpec as P

GROUPS = 4
PER = 4
MEMBERS = 16
DEPTH = 16
SZ = 8
COMP = 8
CY = 32
SEG = 256
LANES = 128
PLANE = COMP * SEG
MAIN = SZ * PLANE
EDGE = MAIN + PLANE
FULL = MAIN + 2 * PLANE
HALO = SZ * COMP * CY
STRIDE = 27 * COMP
VMEM = 40 * 1024 * 1024
F32 = jnp.float32
BF16 = jnp.bfloat16


def params():
    return pltpu.CompilerParams(vmem_limit_bytes=VMEM)


def pack_kernel(main_ref, next_ref, out_ref):
    lane = lax.broadcasted_iota(jnp.int32, (32, LANES), 1)
    for f in range(PER):
        out_ref[0, f, 0:128, :] = main_ref[f, :, 0:LANES]
        out_ref[0, f, 128:256, :] = main_ref[f, :, LANES:SEG]
        after = next_ref[f].astype(F32)
        packed = after[0:32]
        for i in range(1, 4):
            moved = pltpu.roll(after[32 * i : 32 * i + 32], 32 * i, 1)
            packed = jnp.where(lane < 32 * i, packed, moved)
        out_ref[0, f, 256:288, :] = packed.astype(BF16)


def pack(coefficients):
    rows = coefficients.reshape(PER, DEPTH * COMP, GROUPS * SEG)
    return pl.pallas_call(
        pack_kernel,
        grid=(GROUPS,),
        in_specs=[
            pl.BlockSpec((PER, DEPTH * COMP, SEG), lambda d: (0, 0, d)),
            pl.BlockSpec((PER, DEPTH * COMP, LANES), lambda d: (0, 0, jnp.minimum(2 * d + 2, 7))),
        ],
        out_specs=pl.BlockSpec((1, PER, 288, LANES), lambda d: (d, 0, 0, 0)),
        out_shape=jax.ShapeDtypeStruct((GROUPS, PER, 288, LANES), BF16),
        compiler_params=params(),
    )(rows, rows)


def place_kernel(start_ref, extent_ref, in_ref, low_ref, mid_ref, up_ref, s0, s1, sh):
    zero = jnp.zeros((STRIDE, LANES), F32)
    row = lax.broadcasted_iota(jnp.int32, (128, LANES), 0)
    lane16 = lax.broadcasted_iota(jnp.int32, (16, LANES), 1)

    def spread(n, carry):
        base = pl.multiple_of(n * STRIDE, 8)
        for s in (s0, s1, sh):
            s[pl.ds(base, STRIDE), :] = zero
        at = pl.multiple_of(base + start_ref[n] * COMP, 8)
        inside = row < extent_ref[n] * COMP
        s0[pl.ds(at, 128), :] = jnp.where(inside, in_ref[n, 0:128, :].astype(F32), 0.0)
        s1[pl.ds(at, 128), :] = jnp.where(inside, in_ref[n, 128:256, :].astype(F32), 0.0)
        packed = in_ref[n, 256:288, :].astype(F32)
        for i in range(4):
            part = packed if i == 0 else pltpu.roll(packed, LANES - 32 * i, 1)
            part = jnp.where(inside[32 * i : 32 * i + 32], part, 0.0)
            sh[pl.ds(pl.multiple_of(at + 32 * i, 8), 32), :] = part
        return carry

    lax.fori_loop(0, MEMBERS, spread, 0)

    def rows_of(s, r):
        a = s[pl.ds(r, 8, stride=STRIDE), :]
        b = s[pl.ds(8 * STRIDE + r, 8, stride=STRIDE), :]
        return jnp.concatenate([a, b], axis=0)

    for f in range(25):
        for c in range(COMP):
            for h, s in ((0, s0), (1, s1)):
                tile = rows_of(s, f * COMP + c).astype(BF16)
                for ref, first, count in ((low_ref, 0, 9), (mid_ref, 7, 10), (up_ref, 15, 9)):
                    q = f - first
                    if 0 <= q < count:
                        at = (q * COMP + c) * SEG + h * LANES
                        ref[:, at : at + LANES] = tile
    for ref, first, base in ((low_ref, 0, EDGE), (mid_ref, 8, FULL), (up_ref, 16, EDGE)):
        for j in range(2):
            for c in range(COMP):
                packed = rows_of(sh, (first + 4 * j) * COMP + c)
                for i in range(1, 4):
                    moved = pltpu.roll(rows_of(sh, (first + 4 * j + i) * COMP + c), 32 * i, 1)
                    packed = jnp.where(lane16 < 32 * i, packed, moved)
                at = base + (j * COMP + c) * LANES
                ref[:, at : at + LANES] = packed.astype(BF16)


def place(starts, extents, got):
    scratch = pltpu.VMEM((MEMBERS * STRIDE, LANES), F32)
    whole = pl.BlockSpec(memory_space=pltpu.VMEM)
    scalars = pl.BlockSpec(memory_space=pltpu.SMEM)
    return pl.pallas_call(
        place_kernel,
        in_specs=[scalars, scalars, whole],
        out_specs=[whole] * 3,
        out_shape=[
            jax.ShapeDtypeStruct((MEMBERS, EDGE + HALO), BF16),
            jax.ShapeDtypeStruct((MEMBERS, FULL + HALO), BF16),
            jax.ShapeDtypeStruct((MEMBERS, EDGE + HALO), BF16),
        ],
        scratch_shapes=[scratch] * 3,
        compiler_params=params(),
    )(starts, extents, got.reshape(MEMBERS, 288, LANES))


def signed_sums(values):
    values = list(values)
    for bit in (1, 2, 4):
        values = [
            values[k ^ bit] - values[k] if k & bit else values[k] + values[k ^ bit]
            for k in range(COMP)
        ]
    return values


def apply_planes(src, dst, row_at, dst_at, dst_lane, where_ref, pot_ref, lap_ref):
    rel = where_ref[pl.ds(row_at, 16), 0:1]
    ext = where_ref[pl.ds(row_at, 16), 1:2]

    def one(q, carry):
        def plane(at, c):
            lanes = pl.multiple_of(at * PLANE + c * SEG, LANES)
            return src[pl.ds(row_at, 16), pl.ds(lanes, SEG)]

        here = [plane(q + 1, c) for c in range(COMP)]
        plane_term = jnp.dot(
            jnp.concatenate(here, axis=0), lap_ref[...], preferred_element_type=F32
        )
        inside = jnp.where((q >= rel) & (q < rel + ext), -0.5, 0.0)
        orbital = [v.astype(F32) for v in here]
        fine = signed_sums(orbital)
        pot = pot_ref[pl.ds(pl.multiple_of(q * COMP, 8), COMP), :]
        back = signed_sums([fine[k] * pot[k : k + 1] for k in range(COMP)])
        for c in range(COMP):
            beside = plane(q, c).astype(F32) + plane(q + 2, c).astype(F32)
            total = plane_term[16 * c : 16 * c + 16] + back[c]
            total += orbital[c] + inside * beside
            lanes = pl.multiple_of(dst_lane + q * PLANE + c * SEG, LANES)
            dst[pl.ds(dst_at, 16), pl.ds(lanes, SEG)] = total.astype(BF16)
        return carry

    lax.fori_loop(0, SZ, one, 0)


def middle_kernel(mid_ref, where_ref, pot_ref, lap_ref, out_ref):
    apply_planes(mid_ref, out_ref, 0, 0, 0, where_ref, pot_ref, lap_ref)


def middle(mid, where, pot, laplace):
    return pl.pallas_call(
        middle_kernel,
        out_shape=jax.ShapeDtypeStruct((MEMBERS, MAIN), BF16),
        compiler_params=params(),
        cost_estimate=pl.CostEstimate(flops=40_000_000, bytes_accessed=6_000_000, transcendentals=0),
    )(mid, where, pot, laplace)


CONTRACT = (((1,), (1,)), ((), ()))


def gram_kernel(
    share_ref, lower_ref, mid_ref, upper_ref, done_ref, where_ref, pot_ref, lap_ref, out_ref, both, last, halo, sums
):
    blank = jnp.zeros((16, PLANE), BF16)
    both[0:16, 0:EDGE] = lower_ref[:, 0:EDGE]
    both[0:16, EDGE:FULL] = blank
    both[16:32, :] = mid_ref[:, 0:FULL]
    both[32:48, 0:PLANE] = blank
    both[32:48, PLANE:FULL] = upper_ref[:, 0:EDGE]
    both[64:80, PLANE:EDGE] = done_ref[...]
    halo[0:16, :] = lower_ref[:, EDGE : EDGE + HALO]
    halo[16:32, :] = mid_ref[:, FULL : FULL + HALO]
    halo[32:48, :] = upper_ref[:, EDGE : EDGE + HALO]
    for at in (0, 32):
        apply_planes(both, both, at, 48 + at, PLANE, where_ref, pot_ref, lap_ref)
    lane = lax.broadcasted_iota(jnp.int32, (48, LANES), 1)
    for j in range(2):
        for c in range(COMP):
            packed = None
            for i in range(4):
                at = PLANE + ((4 * j + i) * COMP + c) * SEG + LANES
                piece = both[0:48, at : at + LANES].astype(F32)
                if i < 3:
                    piece = pltpu.roll(piece, 32 * (i + 1), 1)
                packed = piece if packed is None else jnp.where(lane < 32 * i, packed, piece)
            at = (j * COMP + c) * LANES
            last[:, at : at + LANES] = packed.astype(BF16)

    def step(q, total):
        lanes = pl.ds(pl.multiple_of(PLANE + q * PLANE, LANES), PLANE)
        return total + lax.dot_general(
            both[:, lanes], both[0:48, lanes], CONTRACT, preferred_element_type=F32
        )

    main = lax.fori_loop(0, SZ, step, jnp.zeros((96, 48), F32))
    cross = lax.dot_general(last[...], halo[...], CONTRACT, preferred_element_type=F32)
    cross += lax.dot_general(halo[...], last[...], CONTRACT, preferred_element_type=F32)
    sums[...] = jnp.zeros((96, LANES), F32)
    sums[0:48, 0:48] = main[0:48]
    sums[48:96, 0:48] = main[48:96] + jnp.where(share_ref[0] > 0, -0.5, 0.0) * cross
    sums[0:48, :] = sums[0:48, :] + pltpu.roll(sums[48:96, :], 64, 1)
    for d in range(GROUPS):
        for k in range(3):
            out_ref[d, PER * k : PER * k + PER, :] = sums[16 * k + PER * d : 16 * k + PER * d + PER, :]


def gram(share, lower, mid, upper, done, where, pot, laplace):
    whole = pl.BlockSpec(memory_space=pltpu.VMEM)
    return pl.pallas_call(
        gram_kernel,
        in_specs=[pl.BlockSpec(memory_space=pltpu.SMEM)] + [whole] * 7,
        out_specs=whole,
        out_shape=jax.ShapeDtypeStruct((GROUPS, 3 * PER, LANES), F32),
        scratch_shapes=[
            pltpu.VMEM((96, FULL), BF16),
            pltpu.VMEM((48, HALO), BF16),
            pltpu.VMEM((48, HALO), BF16),
            pltpu.VMEM((96, LANES), F32),
        ],
        compiler_params=params(),
    )(share, lower, mid, upper, done, where, pot, laplace)


def segment_laplace():
    cells = jnp.arange(SEG, dtype=jnp.int32)
    x, y = cells // CY, cells % CY
    step_x = jnp.abs(x[:, None] - x[None, :])
    step_y = jnp.abs(y[:, None] - y[None, :])
    return jnp.where(
        step_x + step_y == 0, 2.0, jnp.where(step_x + step_y == 1, -0.5, 0.0)
    ).astype(BF16)


def shifted(value, axis, steps):
    count = lax.axis_size(axis)
    return lax.ppermute(value, axis, [(i, (i + steps) % count) for i in range(count)])


def local(potential, coefficients, box_center, box_extent):
    slab = lax.axis_index("slab")
    group = lax.axis_index("grp")
    slabs = lax.axis_size("slab")

    def frames(step):
        source = (slab + step) % slabs
        extents = lax.dynamic_slice_in_dim(box_extent, source * MEMBERS, MEMBERS)
        centers = lax.dynamic_slice_in_dim(box_center, source * MEMBERS, MEMBERS)
        return centers - source * SZ - extents // 2 + step * SZ, extents

    around = [frames(step) for step in (-1, 0, 1)]
    where = jnp.stack(
        [jnp.concatenate([r for r, _ in around]), jnp.concatenate([e for _, e in around])], axis=1
    )
    starts, extents = around[1]
    pot = lax.dynamic_slice_in_dim(potential, group * SEG, SEG, axis=2)
    pot = pot.reshape(SZ * COMP, SEG).astype(F32) * (1.0 / COMP)
    laplace = segment_laplace()
    share = (group < GROUPS - 1).astype(jnp.int32).reshape(1)

    got = lax.all_to_all(pack(coefficients), "grp", 0, 0, tiled=True)
    low, mid, up = place(starts + SZ, extents, got)
    lower = shifted(up, "slab", 1)
    upper = shifted(low, "slab", -1)
    done = middle(mid, where[MEMBERS : 2 * MEMBERS], pot, laplace)
    parts = gram(share, lower, mid, upper, done, where, pot, laplace)
    rows = jnp.sum(lax.all_to_all(parts, "grp", 0, 0, tiled=True), axis=0)
    from_above = shifted(rows[0:PER], "slab", -1)
    own = rows[PER : 2 * PER]
    from_below = shifted(rows[2 * PER :], "slab", 1)

    def band(first):
        out = 0.0
        for block, at in ((from_below, 0), (own, 16), (from_above, 32)):
            out += jnp.pad(block[:, first : first + 48], ((0, 0), (at, 32 - at)))
        return out

    return band(0), band(64)


def solution(mesh):
    return jax.shard_map(
        local,
        mesh=mesh,
        in_specs=(P("slab", None, None), P(("slab", "grp"), None, None, None), P(), P()),
        out_specs=(P(("slab", "grp"), None), P(("slab", "grp"), None)),
        check_vma=False,
    )
```

time: 154 us -> 79.5 us (0.52)
  local copies, waits for them, and re-layouts: 42.6 us -> 1.54 us
  starting transfers between devices: 52.8 us -> 31.3 us
  matrix products: 18.5 us -> 0 us
  Pallas kernels: 0 us -> 13.2 us
  waiting for transfers between devices: 25.7 us -> 21.3 us
  other arithmetic: 4.94 us -> 3.22 us
    ppermute x10 -> x4, starting transfers between devices: 48 us -> 21.9 us  [shifted(): lax.ppermute(value, axis, [(i, (i + steps) % count) for i in range(count)])]
    dot_general x11 -> x0, matrix products: 18.5 us -> none  [the longest x1 5.16 us: apply_hamiltonian(): jnp.dot(orbital.reshape(-1, cell_count), laplace_plane(), preferred_eleme...]
    unnamed x4, local copies, waits for them, and re-layouts: 16.5 us -> 1.22 us
    concatenate x1 -> x0, local copies, waits for them, and re-layouts: 13.6 us -> none  [in_one_piece(): both = jnp.concatenate(arrays, axis=along)]
    pallas_call x0 -> x4, Pallas kernels: none -> 13.2 us  [the longest x1 6.31 us: gram(): pl.pallas_call(gram_kernel, in_specs=[pl.BlockSpec(memory_space=pltpu.SME...]
    all_to_all x1, waiting for transfers between devices: 19.1 us -> 9.61 us  [local(): got = lax.all_to_all(pack(coefficients), 'grp', 0, 0, tiled=True)]
    all_to_all x1 -> x0, local copies, waits for them, and re-layouts: 8.96 us -> none  [in_one_piece(): lax.all_to_all(both, axis, split_axis=split_dim, concat_axis=concat_dim,...]
    ppermute x10 -> x4, waiting for transfers between devices: 6.61 us -> 11.7 us  [shifted(): lax.ppermute(value, axis, [(i, (i + steps) % count) for i in range(count)])]
  transfers between devices with their start and end apart: 11 -> 5, of which waited for: 4 -> 4; matrix products, arithmetic and copies ran while one was open for 12% -> 3% of each run, Pallas kernels for 0% -> 2%
where the time goes in v1:
time: 79.5 us; the launch traced here: 79.1 us
  starting transfers between devices  31.3 us (39%)
  waiting for transfers between devices  21.3 us (27%)
  Pallas kernels  13.2 us (17%)
  blocking collectives  7.81 us (10%)
  other arithmetic  3.22 us (4%)
  local copies, waits for them, and re-layouts  1.54 us (2%)
    ppermute x4, starting transfers between devices, shifted(): lax.ppermute(value, axis, [(i, (i + steps) % count) for i in range(count)])  21.9 us
    ppermute x4, waiting for transfers between devices, shifted(): lax.ppermute(value, axis, [(i, (i + steps) % count) for i in range(count)])  11.7 us
    all_to_all x1, waiting for transfers between devices, local(): got = lax.all_to_all(pack(coefficients), 'grp', 0, 0, tiled=True)  9.61 us
    all_to_all x1, starting transfers between devices, local(): got = lax.all_to_all(pack(coefficients), 'grp', 0, 0, tiled=True)  9.4 us
    all_to_all x1, blocking collectives, local(): rows = jnp.sum(lax.all_to_all(parts, 'grp', 0, 0, tiled=True), axis=0)  7.81 us
    pallas_call x1, Pallas kernels, gram(): pl.pallas_call(gram_kernel, in_specs=[pl.BlockSpec(memory_space=pltpu.SME...  6.31 us
    pallas_call x1, Pallas kernels, place(): pl.pallas_call(place_kernel, in_specs=[scalars, scalars, whole], out_spec...  3.49 us
    pallas_call x1, Pallas kernels, pack(): pl.pallas_call(pack_kernel, grid=(GROUPS,), in_specs=[pl.BlockSpec((PER,...  1.97 us
  transfers between devices with their start and end apart: 5, of which 4 were waited for; matrix products, arithmetic and copies ran while one was open for 3% of the time, Pallas kernels for 2%

profile of v1, /device:TPU:2, one launch (start us, length us, event | category | flops | bytes accessed | tf_op | source)
XLA Modules:
  0.0 79.1 jit_solution(2285569451601512623)
XLA Ops:
  0.6 0.0 copy-start
  0.6 1.2 %copy-done = bf16[4,16,8,1024]{3,2,1,0:T(8,128)(2,1)S(1)} copy-done((bf16[4,16,8,1024]{3,2,1,0:T(8,128)(2,1)S(1)}, bf16[4,16,8,1024]{3,2,1,0:T(8,128)(2,1)}, u32[]{:S(2)}) %copy-start) | copy-done | bytes 1048600
  1.9 2.0 %shard_map.59 = bf16[4,4,288,128]{3,2,1,0:T(8,128)(2,1)} custom-call(bf16[4,128,1024]{2,1,0:T(8,128)(2,1)S(1)} %bitcast.10, bf16[4,128,1024]{2,1,0:T(8,128)(2,1)S(1)} %bitcast.11), custom_call_target="tpu_custom_call" | custom-call | tf_op jit(solution)/shard_map/pallas_call | solution.py:47
  3.8 9.4 %all-to-all-start = ((bf16[4,4,288,128]{3,2,1,0:T(8,128)(2,1)}), bf16[4,4,288,128]{3,2,1,0:T(8,128)(2,1)S(1)}, u32[]{:S(2)}, u32[]{:S(2)}) async-start(bf16[4,4,288,128]{3,2,1,0:T(8,128)(2,1)} %shard_map.59), calls=%async_computation | async-start | bytes 2359296 | tf_op jit(solution)/shard_map/all_to_all | solution.py:279
  13.2 0.9 %subtract_add_fusion.1 = (s32[16]{0:T(128)S(1)}, s32[16]{0:T(128)S(1)}, s32[16]{0:T(128)S(1)}, s32[16]{0:T(128)S(1)}, s32[16]{0:T(128)S(1)}, /*index=5*/s32[16]{0:T(128)S(1)}, s32[16]{0:T(128)S(1)}) fusion(s32[2048]{0:T(1024)} %param.6, s32[]{:T(128)S(6)} %select_n.88, s32[]{:T(128)S(6)} %mul.35, s32[2048]{0:T(1024)} %param.7, s32[]{:T(128)S(6)} %select_n.85, ...), kind=kLoop, calls=%fused_computation.30 | loop fusion | flops 864 | bytes 856 | tf_op jit(solution)/shard_map/add | solution.py:267
  14.1 9.6 %all-to-all-done = bf16[4,4,288,128]{3,2,1,0:T(8,128)(2,1)S(1)} async-done(((bf16[4,4,288,128]{3,2,1,0:T(8,128)(2,1)}), bf16[4,4,288,128]{3,2,1,0:T(8,128)(2,1)S(1)}, u32[]{:S(2)}, u32[]{:S(2)}) %all-to-all-start) | async-done | bytes 1179680 | tf_op jit(solution)/shard_map/all_to_all | solution.py:279
  23.7 3.5 %shard_map.60 = (bf16[16,20480]{1,0:T(8,128)(2,1)S(1)}, bf16[16,22528]{1,0:T(8,128)(2,1)S(1)}, bf16[16,20480]{1,0:T(8,128)(2,1)}) custom-call(s32[16]{0:T(128)S(1)} %get-tuple-element.15.start_ref, s32[16]{0:T(128)S(1)} %get-tuple-element.17.extent_ref, bf16[16,288,128]{2,1,0:T(8,128)(2,1)S(1)} %bitcast.9), custom_call_target="tpu_custom_call" | custom-call | tf_op jit(solution)/shard_map/pallas_call | solution.py:111
  27.2 1.9 %collective-permute-start = (bf16[16,20480]{1,0:T(8,128)(2,1)}, bf16[16,20480]{1,0:T(8,128)(2,1)S(1)}, u32[]{:S(2)}, u32[]{:S(2)}) collective-permute-start(bf16[16,20480]{1,0:T(8,128)(2,1)} %get-tuple-element.5), channel_id=1, source_target_pairs={{0,4},{4,8},{8,12},{12,16},{16,20},{20,24},{24,28},{28,32},{32,36}... | collective-permute-start | bytes 1966088 | tf_op jit(solution)/shard_map/ppermute | solution.py:255
  29.1 12.1 %collective-permute-start.1 = (bf16[16,20480]{1,0:T(8,128)(2,1)S(1)}, bf16[16,20480]{1,0:T(8,128)(2,1)S(1)}, u32[]{:S(2)}, u32[]{:S(2)}) collective-permute-start(bf16[16,20480]{1,0:T(8,128)(2,1)S(1)} %get-tuple-element.7), channel_id=1, source_target_pairs={{0,508},{4,0},{8,4},{12,8},{16,12},{20,16},{24,20},{28,24},{32,28}... | collective-permute-start | bytes 1966088 | tf_op jit(solution)/shard_map/ppermute | solution.py:255
  41.2 0.1 add_bitcast_fusion
  41.3 0.1 copy.8.where_ref
  41.4 0.8 multiply_bitcast_fusion.pot_ref
  42.2 0.2 select_convert_fusion.lap_ref
  42.4 1.4 %shard_map.61.done_ref = bf16[16,16384]{1,0:T(8,128)(2,1)S(1)} custom-call(bf16[16,22528]{1,0:T(8,128)(2,1)S(1)} %get-tuple-element.6.mid_ref, s32[16,2]{1,0:T(8,128)S(1)} %slice.40.where_ref, f32[64,256]{1,0:T(8,128)S(1)} %multiply_bitcast_fusion.pot_ref, bf16[256,256]{1,0:T(8,128)(2,1)S(1)} %select_convert_fusion.lap_ref), custom_call_target="tpu_custom_call" | custom-call | flops 40000000 | bytes 6000000 | tf_op jit(solution)/shard_map/pallas_call | solution.py:169
  43.8 4.0 %collective-permute-done.lower_ref = bf16[16,20480]{1,0:T(8,128)(2,1)S(1)} collective-permute-done((bf16[16,20480]{1,0:T(8,128)(2,1)}, bf16[16,20480]{1,0:T(8,128)(2,1)S(1)}, u32[]{:S(2)}, u32[]{:S(2)}) %collective-permute-start) | collective-permute-done | bytes 655392 | tf_op jit(solution)/shard_map/ppermute | solution.py:255
  47.7 1.5 %collective-permute-done.1.upper_ref = bf16[16,20480]{1,0:T(8,128)(2,1)S(1)} collective-permute-done((bf16[16,20480]{1,0:T(8,128)(2,1)S(1)}, bf16[16,20480]{1,0:T(8,128)(2,1)S(1)}, u32[]{:S(2)}, u32[]{:S(2)}) %collective-permute-start.1) | collective-permute-done | bytes 655392 | tf_op jit(solution)/shard_map/ppermute | solution.py:255
  49.3 0.0 copy-start.1
  49.3 6.3 %shard_map.62 = f32[4,12,128]{2,1,0:T(8,128)S(1)} custom-call(s32[1]{0:T(128)} %bitcast.share_ref, bf16[16,20480]{1,0:T(8,128)(2,1)S(1)} %collective-permute-done.lower_ref, bf16[16,22528]{1,0:T(8,128)(2,1)S(1)} %get-tuple-element.6.mid_ref, bf16[16,20480]{1,0:T(8,128)(2,1)S(1)} %collective-permute-done.1.upper_ref, ...), custom_call_target="tpu_custom_call" | custom-call | tf_op jit(solution)/shard_map/pallas_call | solution.py:228
  55.6 7.8 %all_to_all.10 = f32[4,12,128]{2,1,0:T(8,128)S(1)} all-to-all(f32[4,12,128]{2,1,0:T(8,128)S(1)} %shard_map.62), channel_id=1, replica_groups=mesh['slab'=128,'grp'=4] {'grp'}, dimensions={0} | all-to-all | bytes 49152 | tf_op jit(solution)/shard_map/all_to_all | solution.py:285
  63.4 6.0 %collective-permute-start.3 = (f32[4,128]{1,0:T(4,128)S(1)}, f32[4,128]{1,0:T(4,128)S(1)}, u32[]{:S(2)}, u32[]{:S(2)}) collective-permute-start(f32[4,128]{1,0:T(4,128)S(1)} %get-tuple-element.23), channel_id=1, source_target_pairs={{0,508},{4,0},{8,4},{12,8},{16,12},{20,16},{24,20},{28,24},{32,28}... | collective-permute-start | bytes 6152 | tf_op jit(solution)/shard_map/ppermute | solution.py:255
  69.4 0.1 fusion.6
  69.5 1.9 %collective-permute-start.2 = (f32[4,128]{1,0:T(4,128)S(1)}, f32[4,128]{1,0:T(4,128)S(1)}, u32[]{:S(2)}, u32[]{:S(2)}) collective-permute-start(f32[4,128]{1,0:T(4,128)S(1)} %get-tuple-element.22), channel_id=1, source_target_pairs={{0,4},{4,8},{8,12},{12,16},{16,20},{20,24},{24,28},{28,32},{32,36}... | collective-permute-start | bytes 6152 | tf_op jit(solution)/shard_map/ppermute | solution.py:255
  71.4 0.0 collective-permute-done.3
  71.4 0.1 fusion.8
  71.5 6.2 %collective-permute-done.2 = f32[4,128]{1,0:T(4,128)S(1)} collective-permute-done((f32[4,128]{1,0:T(4,128)S(1)}, f32[4,128]{1,0:T(4,128)S(1)}, u32[]{:S(2)}, u32[]{:S(2)}) %collective-permute-start.2) | collective-permute-done | bytes 2080 | tf_op jit(solution)/shard_map/ppermute | solution.py:255
  77.7 0.1 slice.37
  77.8 0.7 pad_add_fusion
  78.4 0.0 copy-done.1
  78.4 0.7 pad_add_fusion.1
  (5 shorter events, 0.0 us)
Async XLA Ops:
  0.6 1.2 %copy-start = (bf16[4,16,8,1024]{3,2,1,0:T(8,128)(2,1)S(1)}, bf16[4,16,8,1024]{3,2,1,0:T(8,128)(2,1)}, u32[]{:S(2)}) copy-start(bf16[4,16,8,1024]{3,2,1,0:T(8,128)(2,1)} %param.5) | copy-start | bytes 3145732
  3.8 19.9 %all-to-all-start = ((bf16[4,4,288,128]{3,2,1,0:T(8,128)(2,1)}), bf16[4,4,288,128]{3,2,1,0:T(8,128)(2,1)S(1)}, u32[]{:S(2)}, u32[]{:S(2)}) async-start(bf16[4,4,288,128]{3,2,1,0:T(8,128)(2,1)} %shard_map.59), calls=%async_computation | async-start | bytes 2359296 | tf_op jit(solution)/shard_map/all_to_all | solution.py:279
  27.2 20.6 %collective-permute-start = (bf16[16,20480]{1,0:T(8,128)(2,1)}, bf16[16,20480]{1,0:T(8,128)(2,1)S(1)}, u32[]{:S(2)}, u32[]{:S(2)}) collective-permute-start(bf16[16,20480]{1,0:T(8,128)(2,1)} %get-tuple-element.5), channel_id=1, source_target_pairs={{0,4},{4,8},{8,12},{12,16},{16,20},{20,24},{24,28},{28,32},{32,36}... | collective-permute-start | bytes 1966088 | tf_op jit(solution)/shard_map/ppermute | solution.py:255
  29.1 20.2 %collective-permute-start.1 = (bf16[16,20480]{1,0:T(8,128)(2,1)S(1)}, bf16[16,20480]{1,0:T(8,128)(2,1)S(1)}, u32[]{:S(2)}, u32[]{:S(2)}) collective-permute-start(bf16[16,20480]{1,0:T(8,128)(2,1)S(1)} %get-tuple-element.7), channel_id=1, source_target_pairs={{0,508},{4,0},{8,4},{12,8},{16,12},{20,16},{24,20},{28,24},{32,28}... | collective-permute-start | bytes 1966088 | tf_op jit(solution)/shard_map/ppermute | solution.py:255
  49.3 29.1 %copy-start.1 = (pred[80]{0:T(512)(128)(4,1)S(1)}, pred[80]{0:T(512)(128)(4,1)}, u32[]{:S(2)}) copy-start(pred[80]{0:T(512)(128)(4,1)} %constant.98.clone.1) | copy-start | bytes 244
  63.4 8.0 %collective-permute-start.3 = (f32[4,128]{1,0:T(4,128)S(1)}, f32[4,128]{1,0:T(4,128)S(1)}, u32[]{:S(2)}, u32[]{:S(2)}) collective-permute-start(f32[4,128]{1,0:T(4,128)S(1)} %get-tuple-element.23), channel_id=1, source_target_pairs={{0,508},{4,0},{8,4},{12,8},{16,12},{20,16},{24,20},{28,24},{32,28}... | collective-permute-start | bytes 6152 | tf_op jit(solution)/shard_map/ppermute | solution.py:255
  69.5 8.2 %collective-permute-start.2 = (f32[4,128]{1,0:T(4,128)S(1)}, f32[4,128]{1,0:T(4,128)S(1)}, u32[]{:S(2)}, u32[]{:S(2)}) collective-permute-start(f32[4,128]{1,0:T(4,128)S(1)} %get-tuple-element.22), channel_id=1, source_target_pairs={{0,4},{4,8},{8,12},{12,16},{16,20},{20,24},{24,28},{28,32},{32,36}... | collective-permute-start | bytes 6152 | tf_op jit(solution)/shard_map/ppermute | solution.py:255

commit v2 on v1

v2 whole, which is shorter than its diff:
```python
import jax
import jax.numpy as jnp
from jax import lax
from jax.experimental import pallas as pl
from jax.experimental.pallas import tpu as pltpu
from jax.sharding import PartitionSpec as P

GROUPS = 4
PER = 4
MEMBERS = 16
DEPTH = 16
SZ = 8
COMP = 8
CY = 32
SEG = 256
LANES = 128
PLANE = COMP * SEG
MAIN = SZ * PLANE
EDGE = MAIN + PLANE
FULL = MAIN + 2 * PLANE
HALO = SZ * COMP * CY
STRIDE = 27 * COMP
VMEM = 20 * 1024 * 1024
F32 = jnp.float32
BF16 = jnp.bfloat16


SMALL = pl.CostEstimate(flops=1, bytes_accessed=1, transcendentals=0)


def params():
    return pltpu.CompilerParams(vmem_limit_bytes=VMEM)


def pack_kernel(in_ref, out_ref, tiles, after, sems):
    nexts = [
        pltpu.make_async_copy(in_ref.at[:, :, pl.ds((d + 1) * SEG, LANES)], after.at[d], sems.at[d])
        for d in range(GROUPS - 1)
    ]
    mains = [
        [
            pltpu.make_async_copy(
                in_ref.at[:, :, pl.ds(d * SEG + h * LANES, LANES)],
                tiles.at[d, :, pl.ds(h * 128, 128), :],
                sems.at[3 + 2 * d + h],
            )
            for h in range(2)
        ]
        for d in range(GROUPS)
    ]
    outs = [pltpu.make_async_copy(tiles.at[d], out_ref.at[d], sems.at[11 + d]) for d in range(GROUPS)]
    for d in range(GROUPS):
        if d < GROUPS - 1:
            nexts[d].start()
        for copy in mains[d]:
            copy.start()
    lane = lax.broadcasted_iota(jnp.int32, (32, LANES), 1)
    for d in range(GROUPS):
        if d < GROUPS - 1:
            nexts[d].wait()
            for f in range(PER):
                rows = after[d, f].astype(F32)
                tile = rows[0:32]
                for i in range(1, 4):
                    moved = pltpu.roll(rows[32 * i : 32 * i + 32], 32 * i, 1)
                    tile = jnp.where(lane < 32 * i, tile, moved)
                tiles[d, f, 256:288, :] = tile.astype(BF16)
        else:
            tiles[d, :, 256:288, :] = jnp.zeros((PER, 32, LANES), BF16)
        for copy in mains[d]:
            copy.wait()
        outs[d].start()
    for copy in outs:
        copy.wait()


def pack(coefficients):
    rows = coefficients.reshape(PER, DEPTH * COMP, GROUPS * SEG)
    return pl.pallas_call(
        pack_kernel,
        in_specs=[pl.BlockSpec(memory_space=pl.ANY)],
        out_specs=pl.BlockSpec(memory_space=pl.ANY),
        out_shape=jax.ShapeDtypeStruct((GROUPS, PER, 288, LANES), BF16),
        scratch_shapes=[
            pltpu.VMEM((GROUPS, PER, 288, LANES), BF16),
            pltpu.VMEM((GROUPS - 1, PER, DEPTH * COMP, LANES), BF16),
            pltpu.SemaphoreType.DMA((15,)),
        ],
        compiler_params=pltpu.CompilerParams(vmem_limit_bytes=60 * 1024 * 1024),
    )(rows)


def rows_of(frames, r):
    a = frames[pl.ds(r, 8, stride=STRIDE), :]
    b = frames[pl.ds(8 * STRIDE + r, 8, stride=STRIDE), :]
    return jnp.concatenate([a, b], axis=0)


def gather(ref, frames, first, planes, halo_first, base):
    s0, s1, sh = frames
    lane = lax.broadcasted_iota(jnp.int32, (MEMBERS, LANES), 1)
    for r in range(planes * COMP):
        for h, s in ((0, s0), (1, s1)):
            ref[:, r * SEG + h * LANES : r * SEG + h * LANES + LANES] = rows_of(s, first + r).astype(BF16)
    for j in range(2):
        for c in range(COMP):
            packed = rows_of(sh, halo_first + 4 * j * COMP + c)
            for i in range(1, 4):
                moved = pltpu.roll(rows_of(sh, halo_first + (4 * j + i) * COMP + c), 32 * i, 1)
                packed = jnp.where(lane < 32 * i, packed, moved)
            at = base + (j * COMP + c) * LANES
            ref[:, at : at + LANES] = packed.astype(BF16)


def place_kernel(odd_ref, start_ref, extent_ref, in_ref, across_ref, s0, s1, sh):
    zero = jnp.zeros((11 * COMP, LANES), F32)
    row = lax.broadcasted_iota(jnp.int32, (128, LANES), 0)

    for n in range(MEMBERS):
        base = n * STRIDE
        for s in (s0, s1, sh):
            s[base : base + 11 * COMP, :] = zero
            s[base + 16 * COMP : base + 27 * COMP, :] = zero
        at = pl.multiple_of(base + start_ref[n] * COMP, 8)
        inside = row < extent_ref[n] * COMP
        s0[pl.ds(at, 128), :] = jnp.where(inside, in_ref[n, 0:128, :].astype(F32), 0.0)
        s1[pl.ds(at, 128), :] = jnp.where(inside, in_ref[n, 128:256, :].astype(F32), 0.0)
        packed = in_ref[n, 256:288, :].astype(F32)
        for i in range(4):
            part = packed if i == 0 else pltpu.roll(packed, LANES - 32 * i, 1)
            part = jnp.where(inside[32 * i : 32 * i + 32], part, 0.0)
            sh[pl.ds(pl.multiple_of(at + 32 * i, 8), 32), :] = part
    odd = odd_ref[0]
    gather(across_ref, (s0, s1, sh), odd * (15 * COMP), 9, odd * (16 * COMP), EDGE)


def place(odd, starts, extents, got):
    whole = pl.BlockSpec(memory_space=pltpu.VMEM)
    scalars = pl.BlockSpec(memory_space=pltpu.SMEM)
    return pl.pallas_call(
        place_kernel,
        in_specs=[scalars] * 3 + [whole],
        out_specs=[whole] * 4,
        out_shape=[jax.ShapeDtypeStruct((MEMBERS, EDGE + HALO), BF16)]
        + [jax.ShapeDtypeStruct((MEMBERS * STRIDE, LANES), F32)] * 3,
        compiler_params=params(),
    )(odd, starts, extents, got.reshape(MEMBERS, 288, LANES))


def place_near_kernel(odd_ref, _across, s0, s1, sh, chip_ref, mid_ref):
    even = 1 - odd_ref[0]
    gather(chip_ref, (s0, s1, sh), even * (15 * COMP), 9, even * (16 * COMP), EDGE)
    gather(mid_ref, (s0, s1, sh), 7 * COMP, 10, 8 * COMP, FULL)


def place_near(odd, across, frames):
    whole = pl.BlockSpec(memory_space=pltpu.VMEM)
    return pl.pallas_call(
        place_near_kernel,
        in_specs=[pl.BlockSpec(memory_space=pltpu.SMEM), pl.BlockSpec(memory_space=pl.ANY)] + [whole] * 3,
        out_specs=[whole] * 2,
        out_shape=[
            jax.ShapeDtypeStruct((MEMBERS, EDGE + HALO), BF16),
            jax.ShapeDtypeStruct((MEMBERS, FULL + HALO), BF16),
        ],
        compiler_params=params(),
        cost_estimate=SMALL,
    )(odd, across, *frames)


def signed_sums(values):
    values = list(values)
    for bit in (1, 2, 4):
        values = [
            values[k ^ bit] - values[k] if k & bit else values[k] + values[k ^ bit]
            for k in range(COMP)
        ]
    return values


def apply_planes(src, src_at, dst, dst_at, where_ref, where_at, pot_ref, lap_ref):
    rel = where_ref[where_at : where_at + 16, 0:1]
    ext = where_ref[where_at : where_at + 16, 1:2]

    for q in range(SZ):

        def plane(at, c):
            lanes = at * PLANE + c * SEG
            return src[src_at : src_at + 16, lanes : lanes + SEG]

        here = [plane(q + 1, c) for c in range(COMP)]
        plane_term = jnp.dot(
            jnp.concatenate(here, axis=0), lap_ref[...], preferred_element_type=F32
        )
        inside = jnp.where((q >= rel) & (q < rel + ext), -0.5, 0.0)
        orbital = [v.astype(F32) for v in here]
        fine = signed_sums(orbital)
        pot = pot_ref[q * COMP : q * COMP + COMP, :]
        back = signed_sums([fine[k] * pot[k : k + 1] for k in range(COMP)])
        for c in range(COMP):
            beside = plane(q, c).astype(F32) + plane(q + 2, c).astype(F32)
            total = plane_term[16 * c : 16 * c + 16] + back[c]
            total += orbital[c] + inside * beside
            lanes = q * PLANE + c * SEG
            dst[dst_at : dst_at + 16, lanes : lanes + SEG] = total.astype(BF16)


def fill(dst, at, src_ref, above):
    blank = jnp.zeros((16, PLANE), BF16)
    dst[at : at + 16, pl.ds(pl.multiple_of(above * PLANE, LANES), EDGE)] = src_ref[:, 0:EDGE]
    dst[at : at + 16, pl.ds(pl.multiple_of((1 - above) * EDGE, LANES), PLANE)] = blank


def last_rows(dst, dst_at, src, rows):
    lane = lax.broadcasted_iota(jnp.int32, (rows, LANES), 1)
    for j in range(2):
        for c in range(COMP):
            packed = None
            for i in range(4):
                at = PLANE + ((4 * j + i) * COMP + c) * SEG + LANES
                piece = src[0:rows, at : at + LANES].astype(F32)
                if i < 3:
                    piece = pltpu.roll(piece, 32 * (i + 1), 1)
                packed = piece if packed is None else jnp.where(lane < 32 * i, packed, piece)
            at = (j * COMP + c) * LANES
            dst[dst_at : dst_at + rows, at : at + LANES] = packed.astype(BF16)


def contract(a, b):
    return lax.dot_general(a, b, (((1,), (1,)), ((), ())), preferred_element_type=F32)


def near_kernel(
    odd_ref, chip_ref, mid_ref, where_ref, pot_ref, lap_ref, both_ref, last_ref, halo_ref, sum_ref, src
):
    fill(src, 0, chip_ref, 1 - odd_ref[0])
    src[16:32, :] = mid_ref[:, 0:FULL]
    both_ref[0:32, :] = src[:, PLANE:EDGE]
    halo_ref[0:16, :] = chip_ref[:, EDGE : EDGE + HALO]
    halo_ref[16:32, :] = mid_ref[:, FULL : FULL + HALO]
    for at in (0, 16):
        apply_planes(src, at, both_ref, 32 + at, where_ref, at, pot_ref, lap_ref)
    last_rows(last_ref, 0, src, 32)

    sum_ref[:, 0:32] = contract(both_ref[...], both_ref[0:32, :])


def near(odd, chip, mid, where, pot, laplace):
    whole = pl.BlockSpec(memory_space=pltpu.VMEM)
    return pl.pallas_call(
        near_kernel,
        in_specs=[pl.BlockSpec(memory_space=pltpu.SMEM)] + [whole] * 5,
        out_specs=[whole] * 4,
        out_shape=[
            jax.ShapeDtypeStruct((64, MAIN), BF16),
            jax.ShapeDtypeStruct((32, HALO), BF16),
            jax.ShapeDtypeStruct((32, HALO), BF16),
            jax.ShapeDtypeStruct((64, LANES), F32),
        ],
        scratch_shapes=[pltpu.VMEM((32, FULL), BF16)],
        compiler_params=params(),
        cost_estimate=SMALL,
    )(odd, chip, mid, where, pot, laplace)


def far_kernel(
    odd_ref, share_ref, across_ref, both_ref, last_ref, halo_ref, sum_ref, where_ref, pot_ref, lap_ref,
    out_ref, src, far, last, halo, sums,
):
    odd = odd_ref[0]
    fill(src, 0, across_ref, odd)
    far[0:16, :] = src[:, PLANE:EDGE]
    halo[0:32, :] = halo_ref[...]
    halo[32:48, :] = across_ref[:, EDGE : EDGE + HALO]
    last[0:32, :] = last_ref[...]
    last_rows(last, 32, src, 16)
    apply_planes(src, 0, far, 16, where_ref, 32, pot_ref, lap_ref)

    rows = contract(far[...], both_ref[0:32, :])
    column = contract(both_ref[...], far[0:16, :])
    corner = contract(far[...], far[0:16, :])
    cross = contract(last[...], halo[...]) + contract(halo[...], last[...])
    cross = jnp.where(share_ref[0] > 0, -0.5, 0.0) * cross
    sums[...] = jnp.zeros((96, LANES), F32)
    for k in range(2):
        at = 48 * k
        sums[at : at + 32, 0:32] = sum_ref[32 * k : 32 * k + 32, 0:32]
        sums[at + 32 : at + 48, 0:32] = rows[16 * k : 16 * k + 16]
        sums[at : at + 32, 32:48] = column[32 * k : 32 * k + 32]
        sums[at + 32 : at + 48, 32:48] = corner[16 * k : 16 * k + 16]
    sums[48:96, 0:48] = sums[48:96, 0:48] + cross
    lane = lax.broadcasted_iota(jnp.int32, (96, LANES), 1)
    table = sums[...]
    chip_up = pltpu.roll(table, 32, 1)
    across_down = pltpu.roll(table, LANES - 32, 1)
    even = jnp.where(lane < 16, across_down, jnp.where(lane < 32, table, chip_up))
    even = jnp.where(lane < 48, even, 0.0)
    table = jnp.where(odd > 0, table, even)
    sums[0:48, :] = table[0:48] + pltpu.roll(table[48:96], 64, 1)
    for x in range(GROUPS):
        here = odd * GROUPS + x
        there = (1 - odd) * GROUPS + x
        out_ref[here, 0:PER, :] = sums[16 + PER * x : 16 + PER * x + PER, :]
        out_ref[here, PER : 2 * PER, :] = sums[32 + PER * x : 32 + PER * x + PER, :]
        out_ref[there, 0:PER, :] = sums[PER * x : PER * x + PER, :]
        out_ref[there, PER : 2 * PER, :] = jnp.zeros((PER, LANES), F32)


def far(odd, share, across, both, last, halo, sums, where, pot, laplace):
    whole = pl.BlockSpec(memory_space=pltpu.VMEM)
    scalar = pl.BlockSpec(memory_space=pltpu.SMEM)
    return pl.pallas_call(
        far_kernel,
        in_specs=[scalar, scalar] + [whole] * 8,
        out_specs=whole,
        out_shape=jax.ShapeDtypeStruct((2 * GROUPS, 2 * PER, LANES), F32),
        scratch_shapes=[
            pltpu.VMEM((16, FULL), BF16),
            pltpu.VMEM((32, MAIN), BF16),
            pltpu.VMEM((48, HALO), BF16),
            pltpu.VMEM((48, HALO), BF16),
            pltpu.VMEM((96, LANES), F32),
        ],
        compiler_params=params(),
    )(odd, share, across, both, last, halo, sums, where, pot, laplace)


def settle_kernel(odd_ref, parts_ref, rows_ref, far_ref):
    odd = odd_ref[0]
    here, there = odd * GROUPS, (1 - odd) * GROUPS
    same, other = parts_ref[here], parts_ref[there]
    for x in range(1, GROUPS):
        same += parts_ref[here + x]
        other += parts_ref[there + x]
    rows_ref[0:8, :] = same
    rows_ref[8:16, :] = other
    far_ref[...] = same[PER:, :]


def settle(odd, parts):
    whole = pl.BlockSpec(memory_space=pltpu.VMEM)
    return pl.pallas_call(
        settle_kernel,
        in_specs=[pl.BlockSpec(memory_space=pltpu.SMEM), whole],
        out_specs=[whole] * 2,
        out_shape=[jax.ShapeDtypeStruct((16, LANES), F32), jax.ShapeDtypeStruct((PER, LANES), F32)],
        compiler_params=pltpu.CompilerParams(vmem_limit_bytes=4 * 1024 * 1024),
    )(odd, parts)


def finish_kernel(odd_ref, rows_ref, far_ref, margin_ref, ham_ref, far):
    odd = odd_ref[0] > 0
    far[...] = jnp.zeros(far.shape, F32)
    far[0:PER, :] = far_ref[...]
    own, chip, across = rows_ref[0:8, :], rows_ref[8:16, :], far[...]
    blocks = (jnp.where(odd, chip, across), own, jnp.where(odd, across, chip))
    lane = lax.broadcasted_iota(jnp.int32, (8, LANES), 1)
    for ref, first in ((margin_ref, 0), (ham_ref, 64)):
        band = jnp.zeros((8, LANES), F32)
        for k in range(3):
            turn = (16 * k - first) % LANES
            value = blocks[k] if turn == 0 else pltpu.roll(blocks[k], turn, 1)
            band += jnp.where((lane >= 16 * k) & (lane < 16 * k + 48), value, 0.0)
        ref[...] = band[0:PER, 0:80]


def finish(odd, rows, far_rows):
    whole = pl.BlockSpec(memory_space=pltpu.VMEM)
    return pl.pallas_call(
        finish_kernel,
        in_specs=[pl.BlockSpec(memory_space=pltpu.SMEM)] + [whole] * 2,
        out_specs=[whole] * 2,
        out_shape=[jax.ShapeDtypeStruct((PER, 80), F32)] * 2,
        scratch_shapes=[pltpu.VMEM((8, LANES), F32)],
        compiler_params=pltpu.CompilerParams(vmem_limit_bytes=4 * 1024 * 1024),
    )(odd, rows, far_rows)


def segment_laplace():
    cells = jnp.arange(SEG, dtype=jnp.int32)
    x, y = cells // CY, cells % CY
    step_x = jnp.abs(x[:, None] - x[None, :])
    step_y = jnp.abs(y[:, None] - y[None, :])
    return jnp.where(
        step_x + step_y == 0, 2.0, jnp.where(step_x + step_y == 1, -0.5, 0.0)
    ).astype(BF16)


def local(potential, coefficients, box_center, box_extent):
    slab = lax.axis_index("slab")
    group = lax.axis_index("grp")
    slabs = lax.axis_size("slab")
    odd = slab % 2
    on_chip = [(s, s ^ 1) for s in range(slabs)]
    across_chips = [(s, (s + 2 * (s % 2) - 1) % slabs) for s in range(slabs)]
    chips = [
        [(2 * c + k) * GROUPS + x for k in range(2) for x in range(GROUPS)] for c in range(slabs // 2)
    ]

    def frames(step):
        source = (slab + step) % slabs
        extents = lax.dynamic_slice_in_dim(box_extent, source * MEMBERS, MEMBERS)
        centers = lax.dynamic_slice_in_dim(box_center, source * MEMBERS, MEMBERS)
        return centers - source * SZ - extents // 2 + step * SZ, extents

    around = [frames(step) for step in (1 - 2 * odd, 0, 2 * odd - 1)]
    where = jnp.stack(
        [jnp.concatenate([r for r, _ in around]), jnp.concatenate([e for _, e in around])], axis=1
    )
    starts, extents = around[1]
    pot = lax.dynamic_slice_in_dim(potential, group * SEG, SEG, axis=2)
    pot = pot.reshape(SZ * COMP, SEG).astype(F32) * (1.0 / COMP)
    laplace = segment_laplace()
    share = (group < GROUPS - 1).astype(jnp.int32).reshape(1)
    flag = odd.astype(jnp.int32).reshape(1)

    got = lax.all_to_all(pack(coefficients), "grp", 0, 0, tiled=True)
    across, *placed = place(flag, starts + SZ, extents, got)
    chip, mid = place_near(flag, across, placed)
    across = lax.ppermute(across, "slab", across_chips)
    chip = lax.ppermute(chip, "slab", on_chip)
    both, last, halo, sums = near(flag, chip, mid, where, pot, laplace)
    parts = far(flag, share, across, both, last, halo, sums, where, pot, laplace)
    parts = lax.all_to_all(
        parts, ("slab", "grp"), 0, 0, tiled=True, axis_index_groups=chips
    )
    rows, far_rows = settle(flag, parts)
    return finish(flag, rows, lax.ppermute(far_rows, "slab", across_chips))


def solution(mesh):
    return jax.shard_map(
        local,
        mesh=mesh,
        in_specs=(P("slab", None, None), P(("slab", "grp"), None, None, None), P(), P()),
        out_specs=(P(("slab", "grp"), None), P(("slab", "grp"), None)),
        check_vma=False,
    )
```

time: 79.5 us -> 63.8 us (0.80)
  waiting for transfers between devices: 21.3 us -> 12.8 us
  Pallas kernels: 13.2 us -> 10.2 us
  local copies, waits for them, and re-layouts: 1.54 us -> 0.09 us
  other arithmetic: 3.22 us -> 1.9 us
  starting transfers between devices: 31.3 us -> 30 us
    ppermute x4 -> x3, waiting for transfers between devices: 11.7 us -> 3.17 us  [the longest x1 1.66 us: local(): return finish(flag, rows, lax.ppermute(far_rows, 'slab', across_chips))]
    pallas_call x4 -> x7, Pallas kernels: 13.2 us -> 10.2 us  [the longest x1 2.32 us: pack(): pl.pallas_call(pack_kernel, in_specs=[pl.BlockSpec(memory_space=pl.ANY)],...]
    ppermute x4 -> x3, starting transfers between devices: 21.9 us -> 20.6 us  [the longest x1 12.1 us: local(): across = lax.ppermute(across, 'slab', across_chips)]
    add x2 -> x0, other arithmetic: 1.31 us -> none  [band(): out += jnp.pad(block[:, first:first + 48], ((0, 0), (at, 32 - at)))]
    unnamed x4 -> x0, local copies, waits for them, and re-layouts: 1.22 us -> none
  transfers between devices with their start and end apart: 5 -> 4, of which waited for: 4 -> 4; matrix products, arithmetic and copies ran while one was open for 3% -> 3% of each run, Pallas kernels for 2% -> 6%
where the time goes in v2:
time: 63.8 us; the launch traced here: 63.4 us
  starting transfers between devices  30 us (47%)
  waiting for transfers between devices  12.8 us (20%)
  Pallas kernels  10.2 us (16%)
  blocking collectives  7.77 us (12%)
  other arithmetic  1.9 us (3%)
  between operations  0.69 us (1%)
    ppermute x1, starting transfers between devices, local(): across = lax.ppermute(across, 'slab', across_chips)  12.1 us
    all_to_all x1, waiting for transfers between devices, local(): got = lax.all_to_all(pack(coefficients), 'grp', 0, 0, tiled=True)  9.6 us
    all_to_all x1, starting transfers between devices, local(): got = lax.all_to_all(pack(coefficients), 'grp', 0, 0, tiled=True)  9.41 us
    all_to_all x1, blocking collectives, local(): lax.all_to_all(parts, ('slab', 'grp'), 0, 0, tiled=True, axis_index_group...  7.77 us
    ppermute x1, starting transfers between devices, local(): return finish(flag, rows, lax.ppermute(far_rows, 'slab', across_chips))  6.55 us
    pallas_call x1, Pallas kernels, pack(): pl.pallas_call(pack_kernel, in_specs=[pl.BlockSpec(memory_space=pl.ANY)],...  2.32 us
    pallas_call x1, Pallas kernels, near(): pl.pallas_call(near_kernel, in_specs=[pl.BlockSpec(memory_space=pltpu.SME...  2.2 us
    pallas_call x1, Pallas kernels, far(): pl.pallas_call(far_kernel, in_specs=[scalar, scalar] + [whole] * 8, out_s...  2.12 us
  transfers between devices with their start and end apart: 4, of which 4 were waited for; matrix products, arithmetic and copies ran while one was open for 3% of the time, Pallas kernels for 6%

profile of v2, /device:TPU:2, one launch (start us, length us, event | category | flops | bytes accessed | tf_op | source)
XLA Modules:
  0.0 63.4 jit_solution(16850754337818045197)
XLA Ops:
  0.6 2.3 %shard_map.59 = bf16[4,4,288,128]{3,2,1,0:T(8,128)(2,1)} custom-call(bf16[4,128,1024]{2,1,0:T(8,128)(2,1)} %bitcast.11), custom_call_target="tpu_custom_call" | custom-call | tf_op jit(solution)/shard_map/pallas_call | solution.py:79
  3.0 9.4 %all-to-all-start = ((bf16[4,4,288,128]{3,2,1,0:T(8,128)(2,1)}), bf16[4,4,288,128]{3,2,1,0:T(8,128)(2,1)S(1)}, u32[]{:S(2)}, u32[]{:S(2)}) async-start(bf16[4,4,288,128]{3,2,1,0:T(8,128)(2,1)} %shard_map.59), calls=%async_computation | async-start | bytes 2359296 | tf_op jit(solution)/shard_map/all_to_all | solution.py:417
  12.4 0.9 %subtract_add_fusion.1 = (s32[16]{0:T(128)S(1)}, s32[16]{0:T(128)S(1)}, s32[16]{0:T(128)S(1)}, s32[16]{0:T(128)S(1)}, s32[16]{0:T(128)S(1)}, /*index=5*/s32[16]{0:T(128)S(1)}, s32[16]{0:T(128)S(1)}) fusion(s32[2048]{0:T(1024)} %param.6, s32[]{:T(128)S(6)} %select_n.93, s32[]{:T(128)S(6)} %mul.47, s32[]{:T(128)S(6)} %mul.46, s32[2048]{0:T(1024)} %param.7, ...), kind=kLoop, calls=%fused_computation.28 | loop fusion | flops 864 | bytes 864 | tf_op jit(solution)/shard_map/add | solution.py:404
  13.2 9.6 %all-to-all-done = bf16[4,4,288,128]{3,2,1,0:T(8,128)(2,1)S(1)} async-done(((bf16[4,4,288,128]{3,2,1,0:T(8,128)(2,1)}), bf16[4,4,288,128]{3,2,1,0:T(8,128)(2,1)S(1)}, u32[]{:S(2)}, u32[]{:S(2)}) %all-to-all-start) | async-done | bytes 1179680 | tf_op jit(solution)/shard_map/all_to_all | solution.py:417
  22.8 1.4 %shard_map.60 = (bf16[16,20480]{1,0:T(8,128)(2,1)S(1)}, f32[3456,128]{1,0:T(8,128)S(1)}, f32[3456,128]{1,0:T(8,128)S(1)}, f32[3456,128]{1,0:T(8,128)S(1)}) custom-call(s32[1]{0:T(128)} %bitcast.odd_ref, s32[16]{0:T(128)S(1)} %get-tuple-element.33.start_ref, s32[16]{0:T(128)S(1)} %get-tuple-element.35.extent_ref, bf16[16,288,128]{2,1,0:T(8,128)(2,1)S(1)} %bitcast.10), custom_call_target="tpu_custom_call" | custom-call | tf_op jit(solution)/shard_map/pallas_call | solution.py:140
  24.3 12.1 %collective-permute-start = (bf16[16,20480]{1,0:T(8,128)(2,1)S(1)}, bf16[16,20480]{1,0:T(8,128)(2,1)S(1)}, u32[]{:S(2)}, u32[]{:S(2)}) collective-permute-start(bf16[16,20480]{1,0:T(8,128)(2,1)S(1)} %get-tuple-element.14._across), channel_id=1, source_target_pairs={{0,508},{4,8},{8,4},{12,16},{16,12},{20,24},{24,20},{28,32},{32,28... | collective-permute-start | bytes 1966088 | tf_op jit(solution)/shard_map/ppermute | solution.py:420
  36.4 1.5 %shard_map.61 = (bf16[16,20480]{1,0:T(8,128)(2,1)}, bf16[16,22528]{1,0:T(8,128)(2,1)S(1)}) custom-call(s32[1]{0:T(128)} %bitcast.odd_ref, bf16[16,20480]{1,0:T(8,128)(2,1)S(1)} %get-tuple-element.14._across, f32[3456,128]{1,0:T(8,128)S(1)} %get-tuple-element.15.s0, f32[3456,128]{1,0:T(8,128)S(1)} %get-tuple-element.16.s1, f32[3456,128]{1,0:T(8,128)S(1)} %get-tuple-element.17.sh), custom_call_target="tpu_custom_call" | custom-call | flops 1 | bytes 1 | tf_op jit(solution)/shard_map/pallas_call | solution.py:158
  37.9 1.9 %collective-permute-start.1 = (bf16[16,20480]{1,0:T(8,128)(2,1)}, bf16[16,20480]{1,0:T(8,128)(2,1)S(1)}, u32[]{:S(2)}, u32[]{:S(2)}) collective-permute-start(bf16[16,20480]{1,0:T(8,128)(2,1)} %get-tuple-element.18), channel_id=1, source_target_pairs={{0,4},{4,0},{8,12},{12,8},{16,20},{20,16},{24,28},{28,24},{32,36},... | collective-permute-start | bytes 1966088 | tf_op jit(solution)/shard_map/ppermute | solution.py:421
  39.8 0.1 add_bitcast_fusion
  39.9 0.1 copy.8.where_ref
  40.0 0.8 %multiply_bitcast_fusion.pot_ref = f32[64,256]{1,0:T(8,128)S(1)} fusion(bf16[8,8,1024]{2,1,0:T(8,128)(2,1)} %param.4, s32[]{:T(128)S(6)} %select_n.98), kind=kLoop, calls=%fused_computation.4 | loop fusion | flops 32768 | bytes 98308 | tf_op jit(solution)/shard_map/mul | solution.py:412
  40.8 0.2 select_convert_fusion.lap_ref
  40.9 1.1 %collective-permute-done.1.chip_ref = bf16[16,20480]{1,0:T(8,128)(2,1)S(1)} collective-permute-done((bf16[16,20480]{1,0:T(8,128)(2,1)}, bf16[16,20480]{1,0:T(8,128)(2,1)S(1)}, u32[]{:S(2)}, u32[]{:S(2)}) %collective-permute-start.1) | collective-permute-done | bytes 655392 | tf_op jit(solution)/shard_map/ppermute | solution.py:421
  42.1 2.2 %shard_map.62 = (bf16[64,16384]{1,0:T(8,128)(2,1)S(1)}, bf16[32,2048]{1,0:T(8,128)(2,1)S(1)}, bf16[32,2048]{1,0:T(8,128)(2,1)S(1)}, f32[64,128]{1,0:T(8,128)S(1)}) custom-call(s32[1]{0:T(128)} %bitcast.odd_ref, bf16[16,20480]{1,0:T(8,128)(2,1)S(1)} %collective-permute-done.1.chip_ref, bf16[16,22528]{1,0:T(8,128)(2,1)S(1)} %get-tuple-element.19.mid_ref, ...), custom_call_target="tpu_custom_call" | custom-call | flops 1 | bytes 1 | tf_op jit(solution)/shard_map/pallas_call | solution.py:250
  44.3 0.4 collective-permute-done.across_ref
  44.7 2.1 %shard_map.63 = f32[8,8,128]{2,1,0:T(8,128)S(1)} custom-call(s32[1]{0:T(128)} %bitcast.odd_ref, s32[1]{0:T(128)} %bitcast.1.share_ref, bf16[16,20480]{1,0:T(8,128)(2,1)S(1)} %collective-permute-done.across_ref, bf16[64,16384]{1,0:T(8,128)(2,1)S(1)} %get-tuple-element.20.both_ref, bf16[32,2048]{1,0:T(8,128)(2,1)S(1)} %get-tuple-element.21.last_ref, ...), custom_call_target="tpu_custom_call" | custom-call | tf_op jit(solution)/shard_map/pallas_call | solution.py:312
  46.8 7.8 %all_to_all.10.parts_ref = f32[8,8,128]{2,1,0:T(8,128)S(1)} all-to-all(f32[8,8,128]{2,1,0:T(8,128)S(1)} %shard_map.63), channel_id=1, replica_groups={{0,1,2,3,4,5,6,7},{8,9,10,11,12,13,14,15},{16,17,18,19,20,21,22,23},{24..., dimensions={0} | all-to-all | bytes 65536 | tf_op jit(solution)/shard_map/all_to_all | solution.py:424
  54.5 6.5 %collective-permute-start.2 = (f32[4,128]{1,0:T(4,128)S(1)}, f32[4,128]{1,0:T(4,128)S(1)}, u32[]{:S(2)}, u32[]{:S(2)}) collective-permute-start(f32[4,128]{1,0:T(4,128)S(1)} %get-tuple-element.25), channel_id=1, source_target_pairs={{0,508},{4,8},{8,4},{12,16},{16,12},{20,24},{24,20},{28,32},{32,28... | collective-permute-start | bytes 6152 | tf_op jit(solution)/shard_map/ppermute | solution.py:428
  61.1 1.7 %collective-permute-done.2.far_ref = f32[4,128]{1,0:T(4,128)S(1)} collective-permute-done((f32[4,128]{1,0:T(4,128)S(1)}, f32[4,128]{1,0:T(4,128)S(1)}, u32[]{:S(2)}, u32[]{:S(2)}) %collective-permute-start.2) | collective-permute-done | bytes 2080 | tf_op jit(solution)/shard_map/ppermute | solution.py:428
  62.8 0.7 %shard_map.65 = (f32[4,80]{1,0:T(4,128)}, f32[4,80]{1,0:T(4,128)}) custom-call(s32[1]{0:T(128)} %bitcast.odd_ref, f32[16,128]{1,0:T(8,128)S(1)} %get-tuple-element.24.rows_ref, f32[4,128]{1,0:T(4,128)S(1)} %collective-permute-done.2.far_ref), custom_call_target="tpu_custom_call" | custom-call | tf_op jit(solution)/shard_map/pallas_call | solution.py:369
  (3 shorter events, 0.0 us)
Async XLA Ops:
  3.0 19.9 %all-to-all-start = ((bf16[4,4,288,128]{3,2,1,0:T(8,128)(2,1)}), bf16[4,4,288,128]{3,2,1,0:T(8,128)(2,1)S(1)}, u32[]{:S(2)}, u32[]{:S(2)}) async-start(bf16[4,4,288,128]{3,2,1,0:T(8,128)(2,1)} %shard_map.59), calls=%async_computation | async-start | bytes 2359296 | tf_op jit(solution)/shard_map/all_to_all | solution.py:417
  24.3 20.4 %collective-permute-start = (bf16[16,20480]{1,0:T(8,128)(2,1)S(1)}, bf16[16,20480]{1,0:T(8,128)(2,1)S(1)}, u32[]{:S(2)}, u32[]{:S(2)}) collective-permute-start(bf16[16,20480]{1,0:T(8,128)(2,1)S(1)} %get-tuple-element.14._across), channel_id=1, source_target_pairs={{0,508},{4,8},{8,4},{12,16},{16,12},{20,24},{24,20},{28,32},{32,28... | collective-permute-start | bytes 1966088 | tf_op jit(solution)/shard_map/ppermute | solution.py:420
  37.9 4.2 %collective-permute-start.1 = (bf16[16,20480]{1,0:T(8,128)(2,1)}, bf16[16,20480]{1,0:T(8,128)(2,1)S(1)}, u32[]{:S(2)}, u32[]{:S(2)}) collective-permute-start(bf16[16,20480]{1,0:T(8,128)(2,1)} %get-tuple-element.18), channel_id=1, source_target_pairs={{0,4},{4,0},{8,12},{12,8},{16,20},{20,16},{24,28},{28,24},{32,36},... | collective-permute-start | bytes 1966088 | tf_op jit(solution)/shard_map/ppermute | solution.py:421
  54.5 8.2 %collective-permute-start.2 = (f32[4,128]{1,0:T(4,128)S(1)}, f32[4,128]{1,0:T(4,128)S(1)}, u32[]{:S(2)}, u32[]{:S(2)}) collective-permute-start(f32[4,128]{1,0:T(4,128)S(1)} %get-tuple-element.25), channel_id=1, source_target_pairs={{0,508},{4,8},{8,4},{12,16},{16,12},{20,24},{24,20},{28,32},{32,28... | collective-permute-start | bytes 6152 | tf_op jit(solution)/shard_map/ppermute | solution.py:428

commit v3 on v2

--- a/solution.py
+++ b/solution.py
@@ -16,8 +16,7 @@
 LANES = 128
 PLANE = COMP * SEG
 MAIN = SZ * PLANE
-EDGE = MAIN + PLANE
-FULL = MAIN + 2 * PLANE
+FULL = MAIN + PLANE
 HALO = SZ * COMP * CY
 STRIDE = 27 * COMP
 VMEM = 20 * 1024 * 1024
@@ -32,43 +31,37 @@
     return pltpu.CompilerParams(vmem_limit_bytes=VMEM)
 
 
-def pack_kernel(in_ref, out_ref, tiles, after, sems):
-    nexts = [
-        pltpu.make_async_copy(in_ref.at[:, :, pl.ds((d + 1) * SEG, LANES)], after.at[d], sems.at[d])
-        for d in range(GROUPS - 1)
-    ]
+def pack_kernel(in_ref, out_ref, tiles, sems):
     mains = [
         [
             pltpu.make_async_copy(
                 in_ref.at[:, :, pl.ds(d * SEG + h * LANES, LANES)],
                 tiles.at[d, :, pl.ds(h * 128, 128), :],
-                sems.at[3 + 2 * d + h],
+                sems.at[2 * d + h],
             )
             for h in range(2)
         ]
         for d in range(GROUPS)
     ]
-    outs = [pltpu.make_async_copy(tiles.at[d], out_ref.at[d], sems.at[11 + d]) for d in range(GROUPS)]
-    for d in range(GROUPS):
-        if d < GROUPS - 1:
-            nexts[d].start()
+    outs = [pltpu.make_async_copy(tiles.at[d], out_ref.at[d], sems.at[8 + d]) for d in range(GROUPS)]
+    order = range(GROUPS - 1, -1, -1)
+    for d in order:
         for copy in mains[d]:
             copy.start()
     lane = lax.broadcasted_iota(jnp.int32, (32, LANES), 1)
-    for d in range(GROUPS):
-        if d < GROUPS - 1:
-            nexts[d].wait()
+    for d in order:
+        for copy in mains[d]:
+            copy.wait()
+        if d == GROUPS - 1:
+            tiles[d, :, 256:288, :] = jnp.zeros((PER, 32, LANES), BF16)
+        else:
             for f in range(PER):
-                rows = after[d, f].astype(F32)
+                rows = tiles[d + 1, f, 0:128, :].astype(F32)
                 tile = rows[0:32]
                 for i in range(1, 4):
                     moved = pltpu.roll(rows[32 * i : 32 * i + 32], 32 * i, 1)
                     tile = jnp.where(lane < 32 * i, tile, moved)
                 tiles[d, f, 256:288, :] = tile.astype(BF16)
-        else:
-            tiles[d, :, 256:288, :] = jnp.zeros((PER, 32, LANES), BF16)
-        for copy in mains[d]:
-            copy.wait()
         outs[d].start()
     for copy in outs:
         copy.wait()
@@ -83,8 +76,7 @@
         out_shape=jax.ShapeDtypeStruct((GROUPS, PER, 288, LANES), BF16),
         scratch_shapes=[
             pltpu.VMEM((GROUPS, PER, 288, LANES), BF16),
-            pltpu.VMEM((GROUPS - 1, PER, DEPTH * COMP, LANES), BF16),
-            pltpu.SemaphoreType.DMA((15,)),
+            pltpu.SemaphoreType.DMA((12,)),
         ],
         compiler_params=pltpu.CompilerParams(vmem_limit_bytes=60 * 1024 * 1024),
     )(rows)
@@ -113,15 +105,18 @@
 
 
 def place_kernel(odd_ref, start_ref, extent_ref, in_ref, across_ref, s0, s1, sh):
-    zero = jnp.zeros((11 * COMP, LANES), F32)
+    zero = jnp.zeros((COMP, LANES), F32)
     row = lax.broadcasted_iota(jnp.int32, (128, LANES), 0)
 
     for n in range(MEMBERS):
         base = n * STRIDE
-        for s in (s0, s1, sh):
-            s[base : base + 11 * COMP, :] = zero
-            s[base + 16 * COMP : base + 27 * COMP, :] = zero
-        at = pl.multiple_of(base + start_ref[n] * COMP, 8)
+        start = start_ref[n]
+        for i in range(11):
+            blank = start + 16 + i
+            blank = jnp.where(blank < 27, blank, blank - 27)
+            for s in (s0, s1, sh):
+                s[pl.ds(pl.multiple_of(base + blank * COMP, 8), COMP), :] = zero
+        at = pl.multiple_of(base + start * COMP, 8)
         inside = row < extent_ref[n] * COMP
         s0[pl.ds(at, 128), :] = jnp.where(inside, in_ref[n, 0:128, :].astype(F32), 0.0)
         s1[pl.ds(at, 128), :] = jnp.where(inside, in_ref[n, 128:256, :].astype(F32), 0.0)
@@ -131,7 +126,7 @@
             part = jnp.where(inside[32 * i : 32 * i + 32], part, 0.0)
             sh[pl.ds(pl.multiple_of(at + 32 * i, 8), 32), :] = part
     odd = odd_ref[0]
-    gather(across_ref, (s0, s1, sh), odd * (15 * COMP), 9, odd * (16 * COMP), EDGE)
+    gather(across_ref, (s0, s1, sh), odd * (15 * COMP), 8, odd * (16 * COMP), MAIN)
 
 
 def place(odd, starts, extents, got):
@@ -141,7 +136,7 @@
         place_kernel,
         in_specs=[scalars] * 3 + [whole],
         out_specs=[whole] * 4,
-        out_shape=[jax.ShapeDtypeStruct((MEMBERS, EDGE + HALO), BF16)]
+        out_shape=[jax.ShapeDtypeStruct((MEMBERS, MAIN + HALO), BF16)]
         + [jax.ShapeDtypeStruct((MEMBERS * STRIDE, LANES), F32)] * 3,
         compiler_params=params(),
     )(odd, starts, extents, got.reshape(MEMBERS, 288, LANES))
@@ -149,8 +144,8 @@
 
 def place_near_kernel(odd_ref, _across, s0, s1, sh, chip_ref, mid_ref):
     even = 1 - odd_ref[0]
-    gather(chip_ref, (s0, s1, sh), even * (15 * COMP), 9, even * (16 * COMP), EDGE)
-    gather(mid_ref, (s0, s1, sh), 7 * COMP, 10, 8 * COMP, FULL)
+    gather(chip_ref, (s0, s1, sh), even * (15 * COMP), 8, even * (16 * COMP), MAIN)
+    gather(mid_ref, (s0, s1, sh), 7 * COMP, 9, 8 * COMP, FULL)
 
 
 def place_near(odd, across, frames):
@@ -160,7 +155,7 @@
         in_specs=[pl.BlockSpec(memory_space=pltpu.SMEM), pl.BlockSpec(memory_space=pl.ANY)] + [whole] * 3,
         out_specs=[whole] * 2,
         out_shape=[
-            jax.ShapeDtypeStruct((MEMBERS, EDGE + HALO), BF16),
+            jax.ShapeDtypeStruct((MEMBERS, MAIN + HALO), BF16),
             jax.ShapeDtypeStruct((MEMBERS, FULL + HALO), BF16),
         ],
         compiler_params=params(),
@@ -182,33 +177,39 @@
     rel = where_ref[where_at : where_at + 16, 0:1]
     ext = where_ref[where_at : where_at + 16, 1:2]
 
-    for q in range(SZ):
-
-        def plane(at, c):
-            lanes = at * PLANE + c * SEG
-            return src[src_at : src_at + 16, lanes : lanes + SEG]
-
-        here = [plane(q + 1, c) for c in range(COMP)]
-        plane_term = jnp.dot(
-            jnp.concatenate(here, axis=0), lap_ref[...], preferred_element_type=F32
-        )
+    def plane(q, c):
+        lanes = (q + 1) * PLANE + c * SEG
+        return src[src_at : src_at + 16, lanes : lanes + SEG]
+
+    for q in range(-1, SZ):
         inside = jnp.where((q >= rel) & (q < rel + ext), -0.5, 0.0)
-        orbital = [v.astype(F32) for v in here]
-        fine = signed_sums(orbital)
-        pot = pot_ref[q * COMP : q * COMP + COMP, :]
-        back = signed_sums([fine[k] * pot[k : k + 1] for k in range(COMP)])
+        if q < 0:
+            totals = [inside * plane(0, c).astype(F32) for c in range(COMP)]
+        else:
+            here = [plane(q, c) for c in range(COMP)]
+            plane_term = jnp.dot(
+                jnp.concatenate(here, axis=0), lap_ref[...], preferred_element_type=F32
+            )
+            orbital = [v.astype(F32) for v in here]
+            fine = signed_sums(orbital)
+            pot = pot_ref[q * COMP : q * COMP + COMP, :]
+            back = signed_sums([fine[k] * pot[k : k + 1] for k in range(COMP)])
+            totals = []
+            for c in range(COMP):
+                beside = plane(q - 1, c).astype(F32)
+                if q < SZ - 1:
+                    beside += plane(q + 1, c).astype(F32)
+                total = plane_term[16 * c : 16 * c + 16] + back[c]
+                totals.append(total + orbital[c] + inside * beside)
         for c in range(COMP):
-            beside = plane(q, c).astype(F32) + plane(q + 2, c).astype(F32)
-            total = plane_term[16 * c : 16 * c + 16] + back[c]
-            total += orbital[c] + inside * beside
-            lanes = q * PLANE + c * SEG
-            dst[dst_at : dst_at + 16, lanes : lanes + SEG] = total.astype(BF16)
+            lanes = (q + 1) * PLANE + c * SEG
+            dst[dst_at : dst_at + 16, lanes : lanes + SEG] = totals[c].astype(BF16)
 
 
 def fill(dst, at, src_ref, above):
     blank = jnp.zeros((16, PLANE), BF16)
-    dst[at : at + 16, pl.ds(pl.multiple_of(above * PLANE, LANES), EDGE)] = src_ref[:, 0:EDGE]
-    dst[at : at + 16, pl.ds(pl.multiple_of((1 - above) * EDGE, LANES), PLANE)] = blank
+    dst[at : at + 16, pl.ds(pl.multiple_of(above * PLANE, LANES), MAIN)] = src_ref[:, 0:MAIN]
+    dst[at : at + 16, pl.ds(pl.multiple_of((1 - above) * MAIN, LANES), PLANE)] = blank
 
 
 def last_rows(dst, dst_at, src, rows):
@@ -230,19 +231,17 @@
     return lax.dot_general(a, b, (((1,), (1,)), ((), ())), preferred_element_type=F32)
 
 
-def near_kernel(
-    odd_ref, chip_ref, mid_ref, where_ref, pot_ref, lap_ref, both_ref, last_ref, halo_ref, sum_ref, src
-):
-    fill(src, 0, chip_ref, 1 - odd_ref[0])
-    src[16:32, :] = mid_ref[:, 0:FULL]
-    both_ref[0:32, :] = src[:, PLANE:EDGE]
-    halo_ref[0:16, :] = chip_ref[:, EDGE : EDGE + HALO]
+def near_kernel(odd_ref, chip_ref, mid_ref, where_ref, pot_ref, lap_ref, both_ref, last_ref, halo_ref, sum_ref):
+    fill(both_ref, 0, chip_ref, 1 - odd_ref[0])
+    both_ref[16:32, :] = mid_ref[:, 0:FULL]
+    halo_ref[0:16, :] = chip_ref[:, MAIN : MAIN + HALO]
     halo_ref[16:32, :] = mid_ref[:, FULL : FULL + HALO]
     for at in (0, 16):
-        apply_planes(src, at, both_ref, 32 + at, where_ref, at, pot_ref, lap_ref)
-    last_rows(last_ref, 0, src, 32)
-
-    sum_ref[:, 0:32] = contract(both_ref[...], both_ref[0:32, :])
+        apply_planes(both_ref, at, both_ref, 32 + at, where_ref, at, pot_ref, lap_ref)
+    last_rows(last_ref, 0, both_ref, 32)
+    sums = contract(both_ref[:, PLANE:FULL], both_ref[0:32, PLANE:FULL])
+    sum_ref[0:32, 0:32] = sums[0:32]
+    sum_ref[32:64, 0:32] = sums[32:64] + contract(both_ref[32:64, 0:PLANE], both_ref[0:32, 0:PLANE])
 
 
 def near(odd, chip, mid, where, pot, laplace):
@@ -252,12 +251,11 @@
         in_specs=[pl.BlockSpec(memory_space=pltpu.SMEM)] + [whole] * 5,
         out_specs=[whole] * 4,
         out_shape=[
-            jax.ShapeDtypeStruct((64, MAIN), BF16),
+            jax.ShapeDtypeStruct((64, FULL), BF16),
             jax.ShapeDtypeStruct((32, HALO), BF16),
             jax.ShapeDtypeStruct((32, HALO), BF16),
             jax.ShapeDtypeStruct((64, LANES), F32),
         ],
-        scratch_shapes=[pltpu.VMEM((32, FULL), BF16)],
         compiler_params=params(),
         cost_estimate=SMALL,
     )(odd, chip, mid, where, pot, laplace)
@@ -265,29 +263,34 @@
 
 def far_kernel(
     odd_ref, share_ref, across_ref, both_ref, last_ref, halo_ref, sum_ref, where_ref, pot_ref, lap_ref,
-    out_ref, src, far, last, halo, sums,
+    out_ref, far, last, halo, sums,
 ):
     odd = odd_ref[0]
-    fill(src, 0, across_ref, odd)
-    far[0:16, :] = src[:, PLANE:EDGE]
+    fill(far, 0, across_ref, odd)
     halo[0:32, :] = halo_ref[...]
-    halo[32:48, :] = across_ref[:, EDGE : EDGE + HALO]
+    halo[32:48, :] = across_ref[:, MAIN : MAIN + HALO]
     last[0:32, :] = last_ref[...]
-    last_rows(last, 32, src, 16)
-    apply_planes(src, 0, far, 16, where_ref, 32, pot_ref, lap_ref)
-
-    rows = contract(far[...], both_ref[0:32, :])
-    column = contract(both_ref[...], far[0:16, :])
-    corner = contract(far[...], far[0:16, :])
+    last_rows(last, 32, far, 16)
+    apply_planes(far, 0, far, 16, where_ref, 32, pot_ref, lap_ref)
+    main, below = slice(PLANE, FULL), slice(0, PLANE)
+    rows = contract(far[:, main], both_ref[0:32, main])
+    column = contract(both_ref[:, main], far[0:16, main])
+    corner = contract(far[:, main], far[0:16, main])
+    rows_below = contract(far[16:32, below], both_ref[0:32, below])
+    column_below = contract(both_ref[32:64, below], far[0:16, below])
+    corner_below = contract(far[16:32, below], far[0:16, below])
+    rows = (rows[0:16], rows[16:32] + rows_below)
+    column = (column[0:32], column[32:64] + column_below)
+    corner = (corner[0:16], corner[16:32] + corner_below)
     cross = contract(last[...], halo[...]) + contract(halo[...], last[...])
     cross = jnp.where(share_ref[0] > 0, -0.5, 0.0) * cross
     sums[...] = jnp.zeros((96, LANES), F32)
     for k in range(2):
         at = 48 * k
         sums[at : at + 32, 0:32] = sum_ref[32 * k : 32 * k + 32, 0:32]
-        sums[at + 32 : at + 48, 0:32] = rows[16 * k : 16 * k + 16]
-        sums[at : at + 32, 32:48] = column[32 * k : 32 * k + 32]
-        sums[at + 32 : at + 48, 32:48] = corner[16 * k : 16 * k + 16]
+        sums[at + 32 : at + 48, 0:32] = rows[k]
+        sums[at : at + 32, 32:48] = column[k]
+        sums[at + 32 : at + 48, 32:48] = corner[k]
     sums[48:96, 0:48] = sums[48:96, 0:48] + cross
     lane = lax.broadcasted_iota(jnp.int32, (96, LANES), 1)
     table = sums[...]
@@ -315,8 +318,7 @@
         out_specs=whole,
         out_shape=jax.ShapeDtypeStruct((2 * GROUPS, 2 * PER, LANES), F32),
         scratch_shapes=[
-            pltpu.VMEM((16, FULL), BF16),
-            pltpu.VMEM((32, MAIN), BF16),
+            pltpu.VMEM((32, FULL), BF16),
             pltpu.VMEM((48, HALO), BF16),
             pltpu.VMEM((48, HALO), BF16),
             pltpu.VMEM((96, LANES), F32),

time: 63.8 us -> 63.2 us (level)
  Pallas kernels: 10.2 us -> 9.38 us
    pallas_call x1, Pallas kernels: 1.48 us -> 0.63 us  [place_near(): pl.pallas_call(place_near_kernel, in_specs=[pl.BlockSpec(memory_space=plt...]
  transfers between devices with their start and end apart: 4 -> 4, of which waited for: 4 -> 4; matrix products, arithmetic and copies ran while one was open for 3% -> 3% of each run, Pallas kernels for 6% -> 4%
where the time goes in v3:
time: 63.2 us; the launch traced here: 62.8 us
  starting transfers between devices  30 us (47%)
  waiting for transfers between devices  13 us (21%)
  Pallas kernels  9.38 us (15%)
  blocking collectives  7.77 us (12%)
  other arithmetic  1.9 us (3%)
  between operations  0.69 us (1%)
    ppermute x1, starting transfers between devices, local(): across = lax.ppermute(across, 'slab', across_chips)  12.1 us
    all_to_all x1, waiting for transfers between devices, local(): got = lax.all_to_all(pack(coefficients), 'grp', 0, 0, tiled=True)  9.6 us
    all_to_all x1, starting transfers between devices, local(): got = lax.all_to_all(pack(coefficients), 'grp', 0, 0, tiled=True)  9.41 us
    all_to_all x1, blocking collectives, local(): lax.all_to_all(parts, ('slab', 'grp'), 0, 0, tiled=True, axis_index_group...  7.77 us
    ppermute x1, starting transfers between devices, local(): return finish(flag, rows, lax.ppermute(far_rows, 'slab', across_chips))  6.55 us
    pallas_call x1, Pallas kernels, far(): pl.pallas_call(far_kernel, in_specs=[scalar, scalar] + [whole] * 8, out_s...  2.32 us
    pallas_call x1, Pallas kernels, pack(): pl.pallas_call(pack_kernel, in_specs=[pl.BlockSpec(memory_space=pl.ANY)],...  2.26 us
    pallas_call x1, Pallas kernels, near(): pl.pallas_call(near_kernel, in_specs=[pl.BlockSpec(memory_space=pltpu.SME...  2.11 us
  transfers between devices with their start and end apart: 4, of which 4 were waited for; matrix products, arithmetic and copies ran while one was open for 3% of the time, Pallas kernels for 4%

profile of v3, /device:TPU:2, one launch (start us, length us, event | category | flops | bytes accessed | tf_op | source)
XLA Modules:
  0.0 62.8 jit_solution(14404533901174409857)
XLA Ops:
  0.6 2.3 %shard_map.59 = bf16[4,4,288,128]{3,2,1,0:T(8,128)(2,1)} custom-call(bf16[4,128,1024]{2,1,0:T(8,128)(2,1)} %bitcast.11), custom_call_target="tpu_custom_call" | custom-call | tf_op jit(solution)/shard_map/pallas_call | solution.py:72
  2.9 9.4 %all-to-all-start = ((bf16[4,4,288,128]{3,2,1,0:T(8,128)(2,1)}), bf16[4,4,288,128]{3,2,1,0:T(8,128)(2,1)S(1)}, u32[]{:S(2)}, u32[]{:S(2)}) async-start(bf16[4,4,288,128]{3,2,1,0:T(8,128)(2,1)} %shard_map.59), calls=%async_computation | async-start | bytes 2359296 | tf_op jit(solution)/shard_map/all_to_all | solution.py:419
  12.3 0.9 %subtract_add_fusion.1 = (s32[16]{0:T(128)S(1)}, s32[16]{0:T(128)S(1)}, s32[16]{0:T(128)S(1)}, s32[16]{0:T(128)S(1)}, s32[16]{0:T(128)S(1)}, /*index=5*/s32[16]{0:T(128)S(1)}, s32[16]{0:T(128)S(1)}) fusion(s32[2048]{0:T(1024)} %param.6, s32[]{:T(128)S(6)} %select_n.93, s32[]{:T(128)S(6)} %mul.47, s32[]{:T(128)S(6)} %mul.46, s32[2048]{0:T(1024)} %param.7, ...), kind=kLoop, calls=%fused_computation.28 | loop fusion | flops 864 | bytes 864 | tf_op jit(solution)/shard_map/add | solution.py:406
  13.2 9.6 %all-to-all-done = bf16[4,4,288,128]{3,2,1,0:T(8,128)(2,1)S(1)} async-done(((bf16[4,4,288,128]{3,2,1,0:T(8,128)(2,1)}), bf16[4,4,288,128]{3,2,1,0:T(8,128)(2,1)S(1)}, u32[]{:S(2)}, u32[]{:S(2)}) %all-to-all-start) | async-done | bytes 1179680 | tf_op jit(solution)/shard_map/all_to_all | solution.py:419
  22.8 1.4 %shard_map.60 = (bf16[16,18432]{1,0:T(8,128)(2,1)S(1)}, f32[3456,128]{1,0:T(8,128)S(1)}, f32[3456,128]{1,0:T(8,128)S(1)}, f32[3456,128]{1,0:T(8,128)S(1)}) custom-call(s32[1]{0:T(128)} %bitcast.odd_ref, s32[16]{0:T(128)S(1)} %get-tuple-element.33.start_ref, s32[16]{0:T(128)S(1)} %get-tuple-element.35.extent_ref, bf16[16,288,128]{2,1,0:T(8,128)(2,1)S(1)} %bitcast.10), custom_call_target="tpu_custom_call" | custom-call | tf_op jit(solution)/shard_map/pallas_call | solution.py:135
  24.2 12.1 %collective-permute-start = (bf16[16,18432]{1,0:T(8,128)(2,1)S(1)}, bf16[16,18432]{1,0:T(8,128)(2,1)S(1)}, u32[]{:S(2)}, u32[]{:S(2)}) collective-permute-start(bf16[16,18432]{1,0:T(8,128)(2,1)S(1)} %get-tuple-element.14._across), channel_id=1, source_target_pairs={{0,508},{4,8},{8,4},{12,16},{16,12},{20,24},{24,20},{28,32},{32,28... | collective-permute-start | bytes 1769480 | tf_op jit(solution)/shard_map/ppermute | solution.py:422
  36.3 0.6 shard_map.61
  36.9 1.9 %collective-permute-start.1 = (bf16[16,18432]{1,0:T(8,128)(2,1)S(1)}, bf16[16,18432]{1,0:T(8,128)(2,1)S(1)}, u32[]{:S(2)}, u32[]{:S(2)}) collective-permute-start(bf16[16,18432]{1,0:T(8,128)(2,1)S(1)} %get-tuple-element.18), channel_id=1, source_target_pairs={{0,4},{4,0},{8,12},{12,8},{16,20},{20,16},{24,28},{28,24},{32,36},... | collective-permute-start | bytes 1769480 | tf_op jit(solution)/shard_map/ppermute | solution.py:423
  38.8 0.1 add_bitcast_fusion
  38.9 0.1 copy.8.where_ref
  39.0 0.8 %multiply_bitcast_fusion.pot_ref = f32[64,256]{1,0:T(8,128)S(1)} fusion(bf16[8,8,1024]{2,1,0:T(8,128)(2,1)} %param.4, s32[]{:T(128)S(6)} %select_n.98), kind=kLoop, calls=%fused_computation.4 | loop fusion | flops 32768 | bytes 98308 | tf_op jit(solution)/shard_map/mul | solution.py:414
  39.8 0.2 select_convert_fusion.lap_ref
  40.0 0.8 %collective-permute-done.1.chip_ref = bf16[16,18432]{1,0:T(8,128)(2,1)S(1)} collective-permute-done((bf16[16,18432]{1,0:T(8,128)(2,1)S(1)}, bf16[16,18432]{1,0:T(8,128)(2,1)S(1)}, u32[]{:S(2)}, u32[]{:S(2)}) %collective-permute-start.1) | collective-permute-done | bytes 589856 | tf_op jit(solution)/shard_map/ppermute | solution.py:423
  40.8 2.1 %shard_map.62 = (bf16[64,18432]{1,0:T(8,128)(2,1)S(1)}, bf16[32,2048]{1,0:T(8,128)(2,1)S(1)}, bf16[32,2048]{1,0:T(8,128)(2,1)S(1)}, f32[64,128]{1,0:T(8,128)S(1)}) custom-call(s32[1]{0:T(128)} %bitcast.odd_ref, bf16[16,18432]{1,0:T(8,128)(2,1)S(1)} %collective-permute-done.1.chip_ref, bf16[16,20480]{1,0:T(8,128)(2,1)S(1)} %get-tuple-element.19.mid_ref, ...), custom_call_target="tpu_custom_call" | custom-call | flops 1 | bytes 1 | tf_op jit(solution)/shard_map/pallas_call | solution.py:249
  42.9 0.9 %collective-permute-done.across_ref = bf16[16,18432]{1,0:T(8,128)(2,1)S(1)} collective-permute-done((bf16[16,18432]{1,0:T(8,128)(2,1)S(1)}, bf16[16,18432]{1,0:T(8,128)(2,1)S(1)}, u32[]{:S(2)}, u32[]{:S(2)}) %collective-permute-start) | collective-permute-done | bytes 589856 | tf_op jit(solution)/shard_map/ppermute | solution.py:422
  43.8 2.3 %shard_map.63 = f32[8,8,128]{2,1,0:T(8,128)S(1)} custom-call(s32[1]{0:T(128)} %bitcast.odd_ref, s32[1]{0:T(128)} %bitcast.1.share_ref, bf16[16,18432]{1,0:T(8,128)(2,1)S(1)} %collective-permute-done.across_ref, bf16[64,18432]{1,0:T(8,128)(2,1)S(1)} %get-tuple-element.20.both_ref, bf16[32,2048]{1,0:T(8,128)(2,1)S(1)} %get-tuple-element.21.last_ref, ...), custom_call_target="tpu_custom_call" | custom-call | tf_op jit(solution)/shard_map/pallas_call | solution.py:315
  46.2 7.8 %all_to_all.10.parts_ref = f32[8,8,128]{2,1,0:T(8,128)S(1)} all-to-all(f32[8,8,128]{2,1,0:T(8,128)S(1)} %shard_map.63), channel_id=1, replica_groups={{0,1,2,3,4,5,6,7},{8,9,10,11,12,13,14,15},{16,17,18,19,20,21,22,23},{24..., dimensions={0} | all-to-all | bytes 65536 | tf_op jit(solution)/shard_map/all_to_all | solution.py:426
  53.9 6.5 %collective-permute-start.2 = (f32[4,128]{1,0:T(4,128)S(1)}, f32[4,128]{1,0:T(4,128)S(1)}, u32[]{:S(2)}, u32[]{:S(2)}) collective-permute-start(f32[4,128]{1,0:T(4,128)S(1)} %get-tuple-element.25), channel_id=1, source_target_pairs={{0,508},{4,8},{8,4},{12,16},{16,12},{20,24},{24,20},{28,32},{32,28... | collective-permute-start | bytes 6152 | tf_op jit(solution)/shard_map/ppermute | solution.py:430
  60.5 1.7 %collective-permute-done.2.far_ref = f32[4,128]{1,0:T(4,128)S(1)} collective-permute-done((f32[4,128]{1,0:T(4,128)S(1)}, f32[4,128]{1,0:T(4,128)S(1)}, u32[]{:S(2)}, u32[]{:S(2)}) %collective-permute-start.2) | collective-permute-done | bytes 2080 | tf_op jit(solution)/shard_map/ppermute | solution.py:430
  62.1 0.7 %shard_map.65 = (f32[4,80]{1,0:T(4,128)}, f32[4,80]{1,0:T(4,128)}) custom-call(s32[1]{0:T(128)} %bitcast.odd_ref, f32[16,128]{1,0:T(8,128)S(1)} %get-tuple-element.24.rows_ref, f32[4,128]{1,0:T(4,128)S(1)} %collective-permute-done.2.far_ref), custom_call_target="tpu_custom_call" | custom-call | tf_op jit(solution)/shard_map/pallas_call | solution.py:371
  (3 shorter events, 0.0 us)
Async XLA Ops:
  2.9 19.9 %all-to-all-start = ((bf16[4,4,288,128]{3,2,1,0:T(8,128)(2,1)}), bf16[4,4,288,128]{3,2,1,0:T(8,128)(2,1)S(1)}, u32[]{:S(2)}, u32[]{:S(2)}) async-start(bf16[4,4,288,128]{3,2,1,0:T(8,128)(2,1)} %shard_map.59), calls=%async_computation | async-start | bytes 2359296 | tf_op jit(solution)/shard_map/all_to_all | solution.py:419
  24.2 19.7 %collective-permute-start = (bf16[16,18432]{1,0:T(8,128)(2,1)S(1)}, bf16[16,18432]{1,0:T(8,128)(2,1)S(1)}, u32[]{:S(2)}, u32[]{:S(2)}) collective-permute-start(bf16[16,18432]{1,0:T(8,128)(2,1)S(1)} %get-tuple-element.14._across), channel_id=1, source_target_pairs={{0,508},{4,8},{8,4},{12,16},{16,12},{20,24},{24,20},{28,32},{32,28... | collective-permute-start | bytes 1769480 | tf_op jit(solution)/shard_map/ppermute | solution.py:422
  36.9 3.9 %collective-permute-start.1 = (bf16[16,18432]{1,0:T(8,128)(2,1)S(1)}, bf16[16,18432]{1,0:T(8,128)(2,1)S(1)}, u32[]{:S(2)}, u32[]{:S(2)}) collective-permute-start(bf16[16,18432]{1,0:T(8,128)(2,1)S(1)} %get-tuple-element.18), channel_id=1, source_target_pairs={{0,4},{4,0},{8,12},{12,8},{16,20},{20,16},{24,28},{28,24},{32,36},... | collective-permute-start | bytes 1769480 | tf_op jit(solution)/shard_map/ppermute | solution.py:423
  53.9 8.2 %collective-permute-start.2 = (f32[4,128]{1,0:T(4,128)S(1)}, f32[4,128]{1,0:T(4,128)S(1)}, u32[]{:S(2)}, u32[]{:S(2)}) collective-permute-start(f32[4,128]{1,0:T(4,128)S(1)} %get-tuple-element.25), channel_id=1, source_target_pairs={{0,508},{4,8},{8,4},{12,16},{16,12},{20,24},{24,20},{28,32},{32,28... | collective-permute-start | bytes 6152 | tf_op jit(solution)/shard_map/ppermute | solution.py:430

commit v4 on v3

--- a/solution.py
+++ b/solution.py
@@ -88,71 +88,79 @@
     return jnp.concatenate([a, b], axis=0)
 
 
-def gather(ref, frames, first, planes, halo_first, base):
-    s0, s1, sh = frames
+def gather(ref, frames, box_ref, first, planes):
+    s0, s1, _ = frames
     lane = lax.broadcasted_iota(jnp.int32, (MEMBERS, LANES), 1)
-    for r in range(planes * COMP):
-        for h, s in ((0, s0), (1, s1)):
-            ref[:, r * SEG + h * LANES : r * SEG + h * LANES + LANES] = rows_of(s, first + r).astype(BF16)
+    start = jnp.broadcast_to(box_ref[:, 0:1], (MEMBERS, LANES))
+    extent = jnp.broadcast_to(box_ref[:, 1:2], (MEMBERS, LANES))
+
+    def inside(f):
+        return (f >= start) & (f < start + extent)
+
+    for q in range(planes):
+        keep = inside(first + q)
+        for c in range(COMP):
+            for h, s in ((0, s0), (1, s1)):
+                at = (q * COMP + c) * SEG + h * LANES
+                tile = rows_of(s, (first + q) * COMP + c)
+                ref[:, at : at + LANES] = jnp.where(keep, tile, 0.0).astype(BF16)
+    return lane, inside
+
+
+def gather_after(ref, sh, lane, inside, first, base):
     for j in range(2):
+        planes = [first + 4 * j + i for i in range(4)]
+        keep = inside(planes[0] + lane // CY)
         for c in range(COMP):
-            packed = rows_of(sh, halo_first + 4 * j * COMP + c)
+            packed = rows_of(sh, planes[0] * COMP + c)
             for i in range(1, 4):
-                moved = pltpu.roll(rows_of(sh, halo_first + (4 * j + i) * COMP + c), 32 * i, 1)
+                moved = pltpu.roll(rows_of(sh, planes[i] * COMP + c), 32 * i, 1)
                 packed = jnp.where(lane < 32 * i, packed, moved)
             at = base + (j * COMP + c) * LANES
-            ref[:, at : at + LANES] = packed.astype(BF16)
-
-
-def place_kernel(odd_ref, start_ref, extent_ref, in_ref, across_ref, s0, s1, sh):
-    zero = jnp.zeros((COMP, LANES), F32)
-    row = lax.broadcasted_iota(jnp.int32, (128, LANES), 0)
-
+            ref[:, at : at + LANES] = jnp.where(keep, packed, 0.0).astype(BF16)
+
+
+def place_kernel(odd_ref, start_ref, box_ref, in_ref, across_ref, s0, s1, sh):
     for n in range(MEMBERS):
-        base = n * STRIDE
-        start = start_ref[n]
-        for i in range(11):
-            blank = start + 16 + i
-            blank = jnp.where(blank < 27, blank, blank - 27)
-            for s in (s0, s1, sh):
-                s[pl.ds(pl.multiple_of(base + blank * COMP, 8), COMP), :] = zero
-        at = pl.multiple_of(base + start * COMP, 8)
-        inside = row < extent_ref[n] * COMP
-        s0[pl.ds(at, 128), :] = jnp.where(inside, in_ref[n, 0:128, :].astype(F32), 0.0)
-        s1[pl.ds(at, 128), :] = jnp.where(inside, in_ref[n, 128:256, :].astype(F32), 0.0)
+        at = pl.multiple_of(n * STRIDE + start_ref[n] * COMP, 8)
+        s0[pl.ds(at, 128), :] = in_ref[n, 0:128, :].astype(F32)
+        s1[pl.ds(at, 128), :] = in_ref[n, 128:256, :].astype(F32)
         packed = in_ref[n, 256:288, :].astype(F32)
         for i in range(4):
             part = packed if i == 0 else pltpu.roll(packed, LANES - 32 * i, 1)
-            part = jnp.where(inside[32 * i : 32 * i + 32], part, 0.0)
             sh[pl.ds(pl.multiple_of(at + 32 * i, 8), 32), :] = part
     odd = odd_ref[0]
-    gather(across_ref, (s0, s1, sh), odd * (15 * COMP), 8, odd * (16 * COMP), MAIN)
-
-
-def place(odd, starts, extents, got):
+    lane, inside = gather(across_ref, (s0, s1, sh), box_ref, odd * 15, 8)
+    gather_after(across_ref, sh, lane, inside, odd * 16, MAIN)
+
+
+def place(odd, starts, box, got):
     whole = pl.BlockSpec(memory_space=pltpu.VMEM)
     scalars = pl.BlockSpec(memory_space=pltpu.SMEM)
     return pl.pallas_call(
         place_kernel,
-        in_specs=[scalars] * 3 + [whole],
+        in_specs=[scalars] * 2 + [whole] * 2,
         out_specs=[whole] * 4,
         out_shape=[jax.ShapeDtypeStruct((MEMBERS, MAIN + HALO), BF16)]
         + [jax.ShapeDtypeStruct((MEMBERS * STRIDE, LANES), F32)] * 3,
         compiler_params=params(),
-    )(odd, starts, extents, got.reshape(MEMBERS, 288, LANES))
-
-
-def place_near_kernel(odd_ref, _across, s0, s1, sh, chip_ref, mid_ref):
+    )(odd, starts, box, got.reshape(MEMBERS, 288, LANES))
+
+
+def place_near_kernel(odd_ref, box_ref, _across, s0, s1, sh, chip_ref, mid_ref):
     even = 1 - odd_ref[0]
-    gather(chip_ref, (s0, s1, sh), even * (15 * COMP), 8, even * (16 * COMP), MAIN)
-    gather(mid_ref, (s0, s1, sh), 7 * COMP, 9, 8 * COMP, FULL)
-
-
-def place_near(odd, across, frames):
+    frames = (s0, s1, sh)
+    lane, inside = gather(chip_ref, frames, box_ref, even * 15, 8)
+    gather_after(chip_ref, sh, lane, inside, even * 16, MAIN)
+    gather(mid_ref, frames, box_ref, 7, 9)
+    gather_after(mid_ref, sh, lane, inside, 8, FULL)
+
+
+def place_near(odd, box, across, frames):
     whole = pl.BlockSpec(memory_space=pltpu.VMEM)
     return pl.pallas_call(
         place_near_kernel,
-        in_specs=[pl.BlockSpec(memory_space=pltpu.SMEM), pl.BlockSpec(memory_space=pl.ANY)] + [whole] * 3,
+        in_specs=[pl.BlockSpec(memory_space=pltpu.SMEM), whole, pl.BlockSpec(memory_space=pl.ANY)] + [whole] * 3,
         out_specs=[whole] * 2,
         out_shape=[
             jax.ShapeDtypeStruct((MEMBERS, MAIN + HALO), BF16),
@@ -160,7 +168,7 @@
         ],
         compiler_params=params(),
         cost_estimate=SMALL,
-    )(odd, across, *frames)
+    )(odd, box, across, *frames)
 
 
 def signed_sums(values):
@@ -200,7 +208,7 @@
                 if q < SZ - 1:
                     beside += plane(q + 1, c).astype(F32)
                 total = plane_term[16 * c : 16 * c + 16] + back[c]
-                totals.append(total + orbital[c] + inside * beside)
+                totals.append(total + inside * beside)
         for c in range(COMP):
             lanes = (q + 1) * PLANE + c * SEG
             dst[dst_at : dst_at + 16, lanes : lanes + SEG] = totals[c].astype(BF16)
@@ -263,7 +271,7 @@
 
 def far_kernel(
     odd_ref, share_ref, across_ref, both_ref, last_ref, halo_ref, sum_ref, where_ref, pot_ref, lap_ref,
-    out_ref, far, last, halo, sums,
+    out_ref, far, last, halo, sums, turn,
 ):
     odd = odd_ref[0]
     fill(far, 0, across_ref, odd)
@@ -273,15 +281,15 @@
     last_rows(last, 32, far, 16)
     apply_planes(far, 0, far, 16, where_ref, 32, pot_ref, lap_ref)
     main, below = slice(PLANE, FULL), slice(0, PLANE)
-    rows = contract(far[:, main], both_ref[0:32, main])
-    column = contract(both_ref[:, main], far[0:16, main])
-    corner = contract(far[:, main], far[0:16, main])
-    rows_below = contract(far[16:32, below], both_ref[0:32, below])
-    column_below = contract(both_ref[32:64, below], far[0:16, below])
-    corner_below = contract(far[16:32, below], far[0:16, below])
-    rows = (rows[0:16], rows[16:32] + rows_below)
-    column = (column[0:32], column[32:64] + column_below)
-    corner = (corner[0:16], corner[16:32] + corner_below)
+    table = contract(jnp.concatenate([both_ref[:, main], far[:, main]], axis=0), far[:, main])
+    below_table = contract(jnp.concatenate([both_ref[:, below], far[:, below]], axis=0), far[:, below])
+    cols = lax.broadcasted_iota(jnp.int32, (32, 32), 1)
+    turn[...] = jnp.zeros((LANES, LANES), F32)
+    turn[0:32, 0:32] = table[0:32] + jnp.where(cols >= 16, below_table[0:32], 0.0)
+    turned = turn[...].T
+    rows = (turned[0:16, 0:32], turned[16:32, 0:32])
+    column = (table[0:32, 0:16], table[32:64, 0:16] + below_table[32:64, 0:16])
+    corner = (table[64:80, 0:16], table[80:96, 0:16] + below_table[80:96, 0:16])
     cross = contract(last[...], halo[...]) + contract(halo[...], last[...])
     cross = jnp.where(share_ref[0] > 0, -0.5, 0.0) * cross
     sums[...] = jnp.zeros((96, LANES), F32)
@@ -322,6 +330,7 @@
             pltpu.VMEM((48, HALO), BF16),
             pltpu.VMEM((48, HALO), BF16),
             pltpu.VMEM((96, LANES), F32),
+            pltpu.VMEM((LANES, LANES), F32),
         ],
         compiler_params=params(),
     )(odd, share, across, both, last, halo, sums, where, pot, laplace)
@@ -384,7 +393,7 @@
     step_x = jnp.abs(x[:, None] - x[None, :])
     step_y = jnp.abs(y[:, None] - y[None, :])
     return jnp.where(
-        step_x + step_y == 0, 2.0, jnp.where(step_x + step_y == 1, -0.5, 0.0)
+        step_x + step_y == 0, 3.0, jnp.where(step_x + step_y == 1, -0.5, 0.0)
     ).astype(BF16)
 
 
@@ -417,8 +426,9 @@
     flag = odd.astype(jnp.int32).reshape(1)
 
     got = lax.all_to_all(pack(coefficients), "grp", 0, 0, tiled=True)
-    across, *placed = place(flag, starts + SZ, extents, got)
-    chip, mid = place_near(flag, across, placed)
+    box = jnp.stack([starts + SZ, extents], axis=1)
+    across, *placed = place(flag, starts + SZ, box, got)
+    chip, mid = place_near(flag, box, across, placed)
     across = lax.ppermute(across, "slab", across_chips)
     chip = lax.ppermute(chip, "slab", on_chip)
     both, last, halo, sums = near(flag, chip, mid, where, pot, laplace)

time: 63.2 us -> 62.7 us (level)
  transfers between devices with their start and end apart: 4 -> 4, of which waited for: 4 -> 4; matrix products, arithmetic and copies ran while one was open for 3% -> 3% of each run, Pallas kernels for 4% -> 5%
where the time goes in v4:
time: 62.7 us; the launch traced here: 62.3 us
  starting transfers between devices  30 us (48%)
  waiting for transfers between devices  12.8 us (20%)
  Pallas kernels  9.02 us (14%)
  blocking collectives  7.77 us (12%)
  other arithmetic  1.91 us (3%)
  between operations  0.71 us (1%)
    ppermute x1, starting transfers between devices, local(): across = lax.ppermute(across, 'slab', across_chips)  12.1 us
    all_to_all x1, waiting for transfers between devices, local(): got = lax.all_to_all(pack(coefficients), 'grp', 0, 0, tiled=True)  9.5 us
    all_to_all x1, starting transfers between devices, local(): got = lax.all_to_all(pack(coefficients), 'grp', 0, 0, tiled=True)  9.41 us
    all_to_all x1, blocking collectives, local(): lax.all_to_all(parts, ('slab', 'grp'), 0, 0, tiled=True, axis_index_group...  7.77 us
    ppermute x1, starting transfers between devices, local(): return finish(flag, rows, lax.ppermute(far_rows, 'slab', across_chips))  6.55 us
    pallas_call x1, Pallas kernels, pack(): pl.pallas_call(pack_kernel, in_specs=[pl.BlockSpec(memory_space=pl.ANY)],...  2.26 us
    pallas_call x1, Pallas kernels, far(): pl.pallas_call(far_kernel, in_specs=[scalar, scalar] + [whole] * 8, out_s...  2.08 us
    pallas_call x1, Pallas kernels, near(): pl.pallas_call(near_kernel, in_specs=[pl.BlockSpec(memory_space=pltpu.SME...  2.05 us
  transfers between devices with their start and end apart: 4, of which 4 were waited for; matrix products, arithmetic and copies ran while one was open for 3% of the time, Pallas kernels for 5%

profile of v4, /device:TPU:2, one launch (start us, length us, event | category | flops | bytes accessed | tf_op | source)
XLA Modules:
  0.0 62.3 jit_solution(15276601560944534470)
XLA Ops:
  0.6 2.3 %shard_map.59 = bf16[4,4,288,128]{3,2,1,0:T(8,128)(2,1)} custom-call(bf16[4,128,1024]{2,1,0:T(8,128)(2,1)} %bitcast.14), custom_call_target="tpu_custom_call" | custom-call | tf_op jit(solution)/shard_map/pallas_call | solution.py:72
  2.9 9.4 %all-to-all-start = ((bf16[4,4,288,128]{3,2,1,0:T(8,128)(2,1)}), bf16[4,4,288,128]{3,2,1,0:T(8,128)(2,1)S(1)}, u32[]{:S(2)}, u32[]{:S(2)}) async-start(bf16[4,4,288,128]{3,2,1,0:T(8,128)(2,1)} %shard_map.59), calls=%async_computation | async-start | bytes 2359296 | tf_op jit(solution)/shard_map/all_to_all | solution.py:428
  12.3 0.9 %subtract_add_fusion.1 = (s32[16]{0:T(128)S(1)}, s32[16]{0:T(128)S(1)}, s32[16,1]{0,1:T(1,128)S(1)}, s32[16]{0:T(128)S(1)}, s32[16]{0:T(128)S(1)}, /*index=5*/s32[16]{0:T(128)S(1)}, s32[16]{0:T(128)S(1)}) fusion(s32[2048]{0:T(1024)} %param.6, s32[]{:T(128)S(6)} %select_n.93, s32[]{:T(128)S(6)} %mul.47, s32[]{:T(128)S(6)} %mul.46, s32[2048]{0:T(1024)} %param.7, ...), kind=kLoop, calls=%fused_computation.29 | loop fusion | flops 864 | bytes 864 | tf_op jit(solution)/shard_map/add | solution.py:415
  13.2 0.1 copy.10.box_ref
  13.3 9.5 %all-to-all-done = bf16[4,4,288,128]{3,2,1,0:T(8,128)(2,1)S(1)} async-done(((bf16[4,4,288,128]{3,2,1,0:T(8,128)(2,1)}), bf16[4,4,288,128]{3,2,1,0:T(8,128)(2,1)S(1)}, u32[]{:S(2)}, u32[]{:S(2)}) %all-to-all-start) | async-done | bytes 1179680 | tf_op jit(solution)/shard_map/all_to_all | solution.py:428
  22.8 1.1 %shard_map.60 = (bf16[16,18432]{1,0:T(8,128)(2,1)S(1)}, f32[3456,128]{1,0:T(8,128)S(1)}, f32[3456,128]{1,0:T(8,128)S(1)}, f32[3456,128]{1,0:T(8,128)S(1)}) custom-call(s32[1]{0:T(128)} %bitcast.odd_ref, s32[16]{0:T(128)S(1)} %broadcast_add_fusion.start_ref, s32[16,2]{1,0:T(8,128)S(1)} %copy.10.box_ref, bf16[16,288,128]{2,1,0:T(8,128)(2,1)S(1)} %bitcast.13), custom_call_target="tpu_custom_call" | custom-call | tf_op jit(solution)/shard_map/pallas_call | solution.py:140
  23.9 12.1 %collective-permute-start = (bf16[16,18432]{1,0:T(8,128)(2,1)S(1)}, bf16[16,18432]{1,0:T(8,128)(2,1)S(1)}, u32[]{:S(2)}, u32[]{:S(2)}) collective-permute-start(bf16[16,18432]{1,0:T(8,128)(2,1)S(1)} %get-tuple-element.14._across), channel_id=1, source_target_pairs={{0,508},{4,8},{8,4},{12,16},{16,12},{20,24},{24,20},{28,32},{32,28... | collective-permute-start | bytes 1769480 | tf_op jit(solution)/shard_map/ppermute | solution.py:432
  36.0 0.8 %shard_map.61 = (bf16[16,18432]{1,0:T(8,128)(2,1)S(1)}, bf16[16,20480]{1,0:T(8,128)(2,1)S(1)}) custom-call(s32[1]{0:T(128)} %bitcast.odd_ref, s32[16,2]{1,0:T(8,128)S(1)} %copy.10.box_ref, bf16[16,18432]{1,0:T(8,128)(2,1)S(1)} %get-tuple-element.14._across, f32[3456,128]{1,0:T(8,128)S(1)} %get-tuple-element.15.s0, f32[3456,128]{1,0:T(8,128)S(1)} %get-tuple-element.16.s1, ...), custom_call_target="tpu_custom_call" | custom-call | flops 1 | bytes 1 | tf_op jit(solution)/shard_map/pallas_call | solution.py:161
  36.9 1.9 %collective-permute-start.1 = (bf16[16,18432]{1,0:T(8,128)(2,1)S(1)}, bf16[16,18432]{1,0:T(8,128)(2,1)S(1)}, u32[]{:S(2)}, u32[]{:S(2)}) collective-permute-start(bf16[16,18432]{1,0:T(8,128)(2,1)S(1)} %get-tuple-element.18), channel_id=1, source_target_pairs={{0,4},{4,0},{8,12},{12,8},{16,20},{20,16},{24,28},{28,24},{32,36},... | collective-permute-start | bytes 1769480 | tf_op jit(solution)/shard_map/ppermute | solution.py:433
  38.8 0.1 add_bitcast_fusion
  38.9 0.1 copy.12.where_ref
  39.0 0.8 %multiply_bitcast_fusion.pot_ref = f32[64,256]{1,0:T(8,128)S(1)} fusion(bf16[8,8,1024]{2,1,0:T(8,128)(2,1)} %param.4, s32[]{:T(128)S(6)} %select_n.98), kind=kLoop, calls=%fused_computation.4 | loop fusion | flops 32768 | bytes 98308 | tf_op jit(solution)/shard_map/mul | solution.py:423
  39.7 0.2 select_convert_fusion.lap_ref
  39.9 0.8 %collective-permute-done.1.chip_ref = bf16[16,18432]{1,0:T(8,128)(2,1)S(1)} collective-permute-done((bf16[16,18432]{1,0:T(8,128)(2,1)S(1)}, bf16[16,18432]{1,0:T(8,128)(2,1)S(1)}, u32[]{:S(2)}, u32[]{:S(2)}) %collective-permute-start.1) | collective-permute-done | bytes 589856 | tf_op jit(solution)/shard_map/ppermute | solution.py:433
  40.8 2.1 %shard_map.62 = (bf16[64,18432]{1,0:T(8,128)(2,1)S(1)}, bf16[32,2048]{1,0:T(8,128)(2,1)S(1)}, bf16[32,2048]{1,0:T(8,128)(2,1)S(1)}, f32[64,128]{1,0:T(8,128)S(1)}) custom-call(s32[1]{0:T(128)} %bitcast.odd_ref, bf16[16,18432]{1,0:T(8,128)(2,1)S(1)} %collective-permute-done.1.chip_ref, bf16[16,20480]{1,0:T(8,128)(2,1)S(1)} %get-tuple-element.19.mid_ref, ...), custom_call_target="tpu_custom_call" | custom-call | flops 1 | bytes 1 | tf_op jit(solution)/shard_map/pallas_call | solution.py:257
  42.8 0.8 %collective-permute-done.across_ref = bf16[16,18432]{1,0:T(8,128)(2,1)S(1)} collective-permute-done((bf16[16,18432]{1,0:T(8,128)(2,1)S(1)}, bf16[16,18432]{1,0:T(8,128)(2,1)S(1)}, u32[]{:S(2)}, u32[]{:S(2)}) %collective-permute-start) | collective-permute-done | bytes 589856 | tf_op jit(solution)/shard_map/ppermute | solution.py:432
  43.6 2.1 %shard_map.63 = f32[8,8,128]{2,1,0:T(8,128)S(1)} custom-call(s32[1]{0:T(128)} %bitcast.odd_ref, s32[1]{0:T(128)} %bitcast.1.share_ref, bf16[16,18432]{1,0:T(8,128)(2,1)S(1)} %collective-permute-done.across_ref, bf16[64,18432]{1,0:T(8,128)(2,1)S(1)} %get-tuple-element.20.both_ref, bf16[32,2048]{1,0:T(8,128)(2,1)S(1)} %get-tuple-element.21.last_ref, ...), custom_call_target="tpu_custom_call" | custom-call | tf_op jit(solution)/shard_map/pallas_call | solution.py:323
  45.7 7.8 %all_to_all.10.parts_ref = f32[8,8,128]{2,1,0:T(8,128)S(1)} all-to-all(f32[8,8,128]{2,1,0:T(8,128)S(1)} %shard_map.63), channel_id=1, replica_groups={{0,1,2,3,4,5,6,7},{8,9,10,11,12,13,14,15},{16,17,18,19,20,21,22,23},{24..., dimensions={0} | all-to-all | bytes 65536 | tf_op jit(solution)/shard_map/all_to_all | solution.py:436
  53.5 6.5 %collective-permute-start.2 = (f32[4,128]{1,0:T(4,128)S(1)}, f32[4,128]{1,0:T(4,128)S(1)}, u32[]{:S(2)}, u32[]{:S(2)}) collective-permute-start(f32[4,128]{1,0:T(4,128)S(1)} %get-tuple-element.25), channel_id=1, source_target_pairs={{0,508},{4,8},{8,4},{12,16},{16,12},{20,24},{24,20},{28,32},{32,28... | collective-permute-start | bytes 6152 | tf_op jit(solution)/shard_map/ppermute | solution.py:440
  60.0 1.7 %collective-permute-done.2.far_ref = f32[4,128]{1,0:T(4,128)S(1)} collective-permute-done((f32[4,128]{1,0:T(4,128)S(1)}, f32[4,128]{1,0:T(4,128)S(1)}, u32[]{:S(2)}, u32[]{:S(2)}) %collective-permute-start.2) | collective-permute-done | bytes 2080 | tf_op jit(solution)/shard_map/ppermute | solution.py:440
  61.7 0.7 %shard_map.65 = (f32[4,80]{1,0:T(4,128)}, f32[4,80]{1,0:T(4,128)}) custom-call(s32[1]{0:T(128)} %bitcast.odd_ref, f32[16,128]{1,0:T(8,128)S(1)} %get-tuple-element.24.rows_ref, f32[4,128]{1,0:T(4,128)S(1)} %collective-permute-done.2.far_ref), custom_call_target="tpu_custom_call" | custom-call | tf_op jit(solution)/shard_map/pallas_call | solution.py:380
  (5 shorter events, 0.0 us)
Async XLA Ops:
  2.9 19.9 %all-to-all-start = ((bf16[4,4,288,128]{3,2,1,0:T(8,128)(2,1)}), bf16[4,4,288,128]{3,2,1,0:T(8,128)(2,1)S(1)}, u32[]{:S(2)}, u32[]{:S(2)}) async-start(bf16[4,4,288,128]{3,2,1,0:T(8,128)(2,1)} %shard_map.59), calls=%async_computation | async-start | bytes 2359296 | tf_op jit(solution)/shard_map/all_to_all | solution.py:428
  23.9 19.7 %collective-permute-start = (bf16[16,18432]{1,0:T(8,128)(2,1)S(1)}, bf16[16,18432]{1,0:T(8,128)(2,1)S(1)}, u32[]{:S(2)}, u32[]{:S(2)}) collective-permute-start(bf16[16,18432]{1,0:T(8,128)(2,1)S(1)} %get-tuple-element.14._across), channel_id=1, source_target_pairs={{0,508},{4,8},{8,4},{12,16},{16,12},{20,24},{24,20},{28,32},{32,28... | collective-permute-start | bytes 1769480 | tf_op jit(solution)/shard_map/ppermute | solution.py:432
  36.9 3.9 %collective-permute-start.1 = (bf16[16,18432]{1,0:T(8,128)(2,1)S(1)}, bf16[16,18432]{1,0:T(8,128)(2,1)S(1)}, u32[]{:S(2)}, u32[]{:S(2)}) collective-permute-start(bf16[16,18432]{1,0:T(8,128)(2,1)S(1)} %get-tuple-element.18), channel_id=1, source_target_pairs={{0,4},{4,0},{8,12},{12,8},{16,20},{20,16},{24,28},{28,24},{32,36},... | collective-permute-start | bytes 1769480 | tf_op jit(solution)/shard_map/ppermute | solution.py:433
  53.5 8.2 %collective-permute-start.2 = (f32[4,128]{1,0:T(4,128)S(1)}, f32[4,128]{1,0:T(4,128)S(1)}, u32[]{:S(2)}, u32[]{:S(2)}) collective-permute-start(f32[4,128]{1,0:T(4,128)S(1)} %get-tuple-element.25), channel_id=1, source_target_pairs={{0,508},{4,8},{8,4},{12,16},{16,12},{20,24},{24,20},{28,32},{32,28... | collective-permute-start | bytes 6152 | tf_op jit(solution)/shard_map/ppermute | solution.py:440

commit v5 on v4

--- a/solution.py
+++ b/solution.py
@@ -239,7 +239,7 @@
     return lax.dot_general(a, b, (((1,), (1,)), ((), ())), preferred_element_type=F32)
 
 
-def near_kernel(odd_ref, chip_ref, mid_ref, where_ref, pot_ref, lap_ref, both_ref, last_ref, halo_ref, sum_ref):
+def near_kernel(odd_ref, share_ref, chip_ref, mid_ref, where_ref, pot_ref, lap_ref, both_ref, last_ref, halo_ref, sum_ref):
     fill(both_ref, 0, chip_ref, 1 - odd_ref[0])
     both_ref[16:32, :] = mid_ref[:, 0:FULL]
     halo_ref[0:16, :] = chip_ref[:, MAIN : MAIN + HALO]
@@ -249,14 +249,16 @@
     last_rows(last_ref, 0, both_ref, 32)
     sums = contract(both_ref[:, PLANE:FULL], both_ref[0:32, PLANE:FULL])
     sum_ref[0:32, 0:32] = sums[0:32]
-    sum_ref[32:64, 0:32] = sums[32:64] + contract(both_ref[32:64, 0:PLANE], both_ref[0:32, 0:PLANE])
-
-
-def near(odd, chip, mid, where, pot, laplace):
+    below = contract(both_ref[32:64, 0:PLANE], both_ref[0:32, 0:PLANE])
+    cross = contract(last_ref[...], halo_ref[...]) + contract(halo_ref[...], last_ref[...])
+    sum_ref[32:64, 0:32] = sums[32:64] + below + jnp.where(share_ref[0] > 0, -0.5, 0.0) * cross
+
+
+def near(odd, share, chip, mid, where, pot, laplace):
     whole = pl.BlockSpec(memory_space=pltpu.VMEM)
     return pl.pallas_call(
         near_kernel,
-        in_specs=[pl.BlockSpec(memory_space=pltpu.SMEM)] + [whole] * 5,
+        in_specs=[pl.BlockSpec(memory_space=pltpu.SMEM)] * 2 + [whole] * 5,
         out_specs=[whole] * 4,
         out_shape=[
             jax.ShapeDtypeStruct((64, FULL), BF16),
@@ -266,32 +268,32 @@
         ],
         compiler_params=params(),
         cost_estimate=SMALL,
-    )(odd, chip, mid, where, pot, laplace)
+    )(odd, share, chip, mid, where, pot, laplace)
 
 
 def far_kernel(
     odd_ref, share_ref, across_ref, both_ref, last_ref, halo_ref, sum_ref, where_ref, pot_ref, lap_ref,
-    out_ref, far, last, halo, sums, turn,
+    out_ref, far, last, sums, turn,
 ):
     odd = odd_ref[0]
     fill(far, 0, across_ref, odd)
-    halo[0:32, :] = halo_ref[...]
-    halo[32:48, :] = across_ref[:, MAIN : MAIN + HALO]
-    last[0:32, :] = last_ref[...]
-    last_rows(last, 32, far, 16)
+    halo = across_ref[:, MAIN : MAIN + HALO]
+    last_rows(last, 0, far, 16)
     apply_planes(far, 0, far, 16, where_ref, 32, pot_ref, lap_ref)
     main, below = slice(PLANE, FULL), slice(0, PLANE)
     table = contract(jnp.concatenate([both_ref[:, main], far[:, main]], axis=0), far[:, main])
     below_table = contract(jnp.concatenate([both_ref[:, below], far[:, below]], axis=0), far[:, below])
     cols = lax.broadcasted_iota(jnp.int32, (32, 32), 1)
+    factor = jnp.where(share_ref[0] > 0, -0.5, 0.0)
+    cross = factor * (contract(last_ref[...], halo) + contract(halo_ref[...], last[...]))
+    cross_corner = factor * (contract(last[...], halo) + contract(halo, last[...]))
     turn[...] = jnp.zeros((LANES, LANES), F32)
     turn[0:32, 0:32] = table[0:32] + jnp.where(cols >= 16, below_table[0:32], 0.0)
+    turn[0:32, 16:32] = turn[0:32, 16:32] + cross
     turned = turn[...].T
     rows = (turned[0:16, 0:32], turned[16:32, 0:32])
-    column = (table[0:32, 0:16], table[32:64, 0:16] + below_table[32:64, 0:16])
-    corner = (table[64:80, 0:16], table[80:96, 0:16] + below_table[80:96, 0:16])
-    cross = contract(last[...], halo[...]) + contract(halo[...], last[...])
-    cross = jnp.where(share_ref[0] > 0, -0.5, 0.0) * cross
+    column = (table[0:32, 0:16], table[32:64, 0:16] + below_table[32:64, 0:16] + cross)
+    corner = (table[64:80, 0:16], table[80:96, 0:16] + below_table[80:96, 0:16] + cross_corner)
     sums[...] = jnp.zeros((96, LANES), F32)
     for k in range(2):
         at = 48 * k
@@ -299,7 +301,6 @@
         sums[at + 32 : at + 48, 0:32] = rows[k]
         sums[at : at + 32, 32:48] = column[k]
         sums[at + 32 : at + 48, 32:48] = corner[k]
-    sums[48:96, 0:48] = sums[48:96, 0:48] + cross
     lane = lax.broadcasted_iota(jnp.int32, (96, LANES), 1)
     table = sums[...]
     chip_up = pltpu.roll(table, 32, 1)
@@ -327,8 +328,7 @@
         out_shape=jax.ShapeDtypeStruct((2 * GROUPS, 2 * PER, LANES), F32),
         scratch_shapes=[
             pltpu.VMEM((32, FULL), BF16),
-            pltpu.VMEM((48, HALO), BF16),
-            pltpu.VMEM((48, HALO), BF16),
+            pltpu.VMEM((16, HALO), BF16),
             pltpu.VMEM((96, LANES), F32),
             pltpu.VMEM((LANES, LANES), F32),
         ],
@@ -431,7 +431,7 @@
     chip, mid = place_near(flag, box, across, placed)
     across = lax.ppermute(across, "slab", across_chips)
     chip = lax.ppermute(chip, "slab", on_chip)
-    both, last, halo, sums = near(flag, chip, mid, where, pot, laplace)
+    both, last, halo, sums = near(flag, share, chip, mid, where, pot, laplace)
     parts = far(flag, share, across, both, last, halo, sums, where, pot, laplace)
     parts = lax.all_to_all(
         parts, ("slab", "grp"), 0, 0, tiled=True, axis_index_groups=chips

time: 62.7 us -> 62.7 us (level)
  no operation moved by 1% of the time
where the time goes in v5:
time: 62.7 us; the launch traced here: 62.3 us
  starting transfers between devices  30 us (48%)
  waiting for transfers between devices  12.7 us (20%)
  Pallas kernels  9.05 us (14%)
  blocking collectives  7.76 us (12%)
  other arithmetic  1.91 us (3%)
  between operations  0.71 us (1%)
    ppermute x1, starting transfers between devices, local(): across = lax.ppermute(across, 'slab', across_chips)  12.1 us
    all_to_all x1, waiting for transfers between devices, local(): got = lax.all_to_all(pack(coefficients), 'grp', 0, 0, tiled=True)  9.5 us
    all_to_all x1, starting transfers between devices, local(): got = lax.all_to_all(pack(coefficients), 'grp', 0, 0, tiled=True)  9.41 us
    all_to_all x1, blocking collectives, local(): lax.all_to_all(parts, ('slab', 'grp'), 0, 0, tiled=True, axis_index_group...  7.76 us
    ppermute x1, starting transfers between devices, local(): return finish(flag, rows, lax.ppermute(far_rows, 'slab', across_chips))  6.55 us
    pallas_call x1, Pallas kernels, pack(): pl.pallas_call(pack_kernel, in_specs=[pl.BlockSpec(memory_space=pl.ANY)],...  2.26 us
    pallas_call x1, Pallas kernels, near(): pl.pallas_call(near_kernel, in_specs=[pl.BlockSpec(memory_space=pltpu.SME...  2.11 us
    pallas_call x1, Pallas kernels, far(): pl.pallas_call(far_kernel, in_specs=[scalar, scalar] + [whole] * 8, out_s...  2.06 us
  transfers between devices with their start and end apart: 4, of which 4 were waited for; matrix products, arithmetic and copies ran while one was open for 3% of the time, Pallas kernels for 5%

profile of v5, /device:TPU:2, one launch (start us, length us, event | category | flops | bytes accessed | tf_op | source)
XLA Modules:
  0.0 62.3 jit_solution(9193601460095266948)
XLA Ops:
  0.6 2.3 %shard_map.59 = bf16[4,4,288,128]{3,2,1,0:T(8,128)(2,1)} custom-call(bf16[4,128,1024]{2,1,0:T(8,128)(2,1)} %bitcast.14), custom_call_target="tpu_custom_call" | custom-call | tf_op jit(solution)/shard_map/pallas_call | solution.py:72
  2.9 9.4 %all-to-all-start = ((bf16[4,4,288,128]{3,2,1,0:T(8,128)(2,1)}), bf16[4,4,288,128]{3,2,1,0:T(8,128)(2,1)S(1)}, u32[]{:S(2)}, u32[]{:S(2)}) async-start(bf16[4,4,288,128]{3,2,1,0:T(8,128)(2,1)} %shard_map.59), calls=%async_computation | async-start | bytes 2359296 | tf_op jit(solution)/shard_map/all_to_all | solution.py:428
  12.3 0.9 %subtract_add_fusion.1 = (s32[16]{0:T(128)S(1)}, s32[16]{0:T(128)S(1)}, s32[16,1]{0,1:T(1,128)S(1)}, s32[16]{0:T(128)S(1)}, s32[16]{0:T(128)S(1)}, /*index=5*/s32[16]{0:T(128)S(1)}, s32[16]{0:T(128)S(1)}) fusion(s32[2048]{0:T(1024)} %param.6, s32[]{:T(128)S(6)} %select_n.93, s32[]{:T(128)S(6)} %mul.47, s32[]{:T(128)S(6)} %mul.46, s32[2048]{0:T(1024)} %param.7, ...), kind=kLoop, calls=%fused_computation.29 | loop fusion | flops 864 | bytes 864 | tf_op jit(solution)/shard_map/add | solution.py:415
  13.2 0.1 copy.10.box_ref
  13.3 9.5 %all-to-all-done = bf16[4,4,288,128]{3,2,1,0:T(8,128)(2,1)S(1)} async-done(((bf16[4,4,288,128]{3,2,1,0:T(8,128)(2,1)}), bf16[4,4,288,128]{3,2,1,0:T(8,128)(2,1)S(1)}, u32[]{:S(2)}, u32[]{:S(2)}) %all-to-all-start) | async-done | bytes 1179680 | tf_op jit(solution)/shard_map/all_to_all | solution.py:428
  22.8 1.1 %shard_map.60 = (bf16[16,18432]{1,0:T(8,128)(2,1)S(1)}, f32[3456,128]{1,0:T(8,128)S(1)}, f32[3456,128]{1,0:T(8,128)S(1)}, f32[3456,128]{1,0:T(8,128)S(1)}) custom-call(s32[1]{0:T(128)} %bitcast.odd_ref, s32[16]{0:T(128)S(1)} %broadcast_add_fusion.start_ref, s32[16,2]{1,0:T(8,128)S(1)} %copy.10.box_ref, bf16[16,288,128]{2,1,0:T(8,128)(2,1)S(1)} %bitcast.13), custom_call_target="tpu_custom_call" | custom-call | tf_op jit(solution)/shard_map/pallas_call | solution.py:140
  23.9 12.1 %collective-permute-start = (bf16[16,18432]{1,0:T(8,128)(2,1)S(1)}, bf16[16,18432]{1,0:T(8,128)(2,1)S(1)}, u32[]{:S(2)}, u32[]{:S(2)}) collective-permute-start(bf16[16,18432]{1,0:T(8,128)(2,1)S(1)} %get-tuple-element.14._across), channel_id=1, source_target_pairs={{0,508},{4,8},{8,4},{12,16},{16,12},{20,24},{24,20},{28,32},{32,28... | collective-permute-start | bytes 1769480 | tf_op jit(solution)/shard_map/ppermute | solution.py:432
  36.0 0.8 %shard_map.61 = (bf16[16,18432]{1,0:T(8,128)(2,1)S(1)}, bf16[16,20480]{1,0:T(8,128)(2,1)S(1)}) custom-call(s32[1]{0:T(128)} %bitcast.odd_ref, s32[16,2]{1,0:T(8,128)S(1)} %copy.10.box_ref, bf16[16,18432]{1,0:T(8,128)(2,1)S(1)} %get-tuple-element.14._across, f32[3456,128]{1,0:T(8,128)S(1)} %get-tuple-element.15.s0, f32[3456,128]{1,0:T(8,128)S(1)} %get-tuple-element.16.s1, ...), custom_call_target="tpu_custom_call" | custom-call | flops 1 | bytes 1 | tf_op jit(solution)/shard_map/pallas_call | solution.py:161
  36.9 1.9 %collective-permute-start.1 = (bf16[16,18432]{1,0:T(8,128)(2,1)S(1)}, bf16[16,18432]{1,0:T(8,128)(2,1)S(1)}, u32[]{:S(2)}, u32[]{:S(2)}) collective-permute-start(bf16[16,18432]{1,0:T(8,128)(2,1)S(1)} %get-tuple-element.18), channel_id=1, source_target_pairs={{0,4},{4,0},{8,12},{12,8},{16,20},{20,16},{24,28},{28,24},{32,36},... | collective-permute-start | bytes 1769480 | tf_op jit(solution)/shard_map/ppermute | solution.py:433
  38.8 0.1 add_bitcast_fusion
  38.9 0.1 copy.12.where_ref
  39.0 0.8 %multiply_bitcast_fusion.pot_ref = f32[64,256]{1,0:T(8,128)S(1)} fusion(bf16[8,8,1024]{2,1,0:T(8,128)(2,1)} %param.4, s32[]{:T(128)S(6)} %select_n.98), kind=kLoop, calls=%fused_computation.4 | loop fusion | flops 32768 | bytes 98308 | tf_op jit(solution)/shard_map/mul | solution.py:423
  39.7 0.2 select_convert_fusion.lap_ref
  39.9 0.8 %collective-permute-done.1.chip_ref = bf16[16,18432]{1,0:T(8,128)(2,1)S(1)} collective-permute-done((bf16[16,18432]{1,0:T(8,128)(2,1)S(1)}, bf16[16,18432]{1,0:T(8,128)(2,1)S(1)}, u32[]{:S(2)}, u32[]{:S(2)}) %collective-permute-start.1) | collective-permute-done | bytes 589856 | tf_op jit(solution)/shard_map/ppermute | solution.py:433
  40.8 2.1 %shard_map.62 = (bf16[64,18432]{1,0:T(8,128)(2,1)S(1)}, bf16[32,2048]{1,0:T(8,128)(2,1)S(1)}, bf16[32,2048]{1,0:T(8,128)(2,1)S(1)}, f32[64,128]{1,0:T(8,128)S(1)}) custom-call(s32[1]{0:T(128)} %bitcast.odd_ref, s32[1]{0:T(128)} %bitcast.1.share_ref, bf16[16,18432]{1,0:T(8,128)(2,1)S(1)} %collective-permute-done.1.chip_ref, ...), custom_call_target="tpu_custom_call" | custom-call | flops 1 | bytes 1 | tf_op jit(solution)/shard_map/pallas_call | solution.py:259
  42.9 0.7 %collective-permute-done.across_ref = bf16[16,18432]{1,0:T(8,128)(2,1)S(1)} collective-permute-done((bf16[16,18432]{1,0:T(8,128)(2,1)S(1)}, bf16[16,18432]{1,0:T(8,128)(2,1)S(1)}, u32[]{:S(2)}, u32[]{:S(2)}) %collective-permute-start) | collective-permute-done | bytes 589856 | tf_op jit(solution)/shard_map/ppermute | solution.py:432
  43.6 2.1 %shard_map.63 = f32[8,8,128]{2,1,0:T(8,128)S(1)} custom-call(s32[1]{0:T(128)} %bitcast.odd_ref, s32[1]{0:T(128)} %bitcast.1.share_ref, bf16[16,18432]{1,0:T(8,128)(2,1)S(1)} %collective-permute-done.across_ref, bf16[64,18432]{1,0:T(8,128)(2,1)S(1)} %get-tuple-element.20.both_ref, bf16[32,2048]{1,0:T(8,128)(2,1)S(1)} %get-tuple-element.21.last_ref, ...), custom_call_target="tpu_custom_call" | custom-call | tf_op jit(solution)/shard_map/pallas_call | solution.py:324
  45.6 7.8 %all_to_all.10.parts_ref = f32[8,8,128]{2,1,0:T(8,128)S(1)} all-to-all(f32[8,8,128]{2,1,0:T(8,128)S(1)} %shard_map.63), channel_id=1, replica_groups={{0,1,2,3,4,5,6,7},{8,9,10,11,12,13,14,15},{16,17,18,19,20,21,22,23},{24..., dimensions={0} | all-to-all | bytes 65536 | tf_op jit(solution)/shard_map/all_to_all | solution.py:436
  53.4 6.6 %collective-permute-start.2 = (f32[4,128]{1,0:T(4,128)S(1)}, f32[4,128]{1,0:T(4,128)S(1)}, u32[]{:S(2)}, u32[]{:S(2)}) collective-permute-start(f32[4,128]{1,0:T(4,128)S(1)} %get-tuple-element.25), channel_id=1, source_target_pairs={{0,508},{4,8},{8,4},{12,16},{16,12},{20,24},{24,20},{28,32},{32,28... | collective-permute-start | bytes 6152 | tf_op jit(solution)/shard_map/ppermute | solution.py:440
  60.0 1.7 %collective-permute-done.2.far_ref = f32[4,128]{1,0:T(4,128)S(1)} collective-permute-done((f32[4,128]{1,0:T(4,128)S(1)}, f32[4,128]{1,0:T(4,128)S(1)}, u32[]{:S(2)}, u32[]{:S(2)}) %collective-permute-start.2) | collective-permute-done | bytes 2080 | tf_op jit(solution)/shard_map/ppermute | solution.py:440
  61.6 0.7 %shard_map.65 = (f32[4,80]{1,0:T(4,128)}, f32[4,80]{1,0:T(4,128)}) custom-call(s32[1]{0:T(128)} %bitcast.odd_ref, f32[16,128]{1,0:T(8,128)S(1)} %get-tuple-element.24.rows_ref, f32[4,128]{1,0:T(4,128)S(1)} %collective-permute-done.2.far_ref), custom_call_target="tpu_custom_call" | custom-call | tf_op jit(solution)/shard_map/pallas_call | solution.py:380
  (5 shorter events, 0.0 us)
Async XLA Ops:
  2.9 19.9 %all-to-all-start = ((bf16[4,4,288,128]{3,2,1,0:T(8,128)(2,1)}), bf16[4,4,288,128]{3,2,1,0:T(8,128)(2,1)S(1)}, u32[]{:S(2)}, u32[]{:S(2)}) async-start(bf16[4,4,288,128]{3,2,1,0:T(8,128)(2,1)} %shard_map.59), calls=%async_computation | async-start | bytes 2359296 | tf_op jit(solution)/shard_map/all_to_all | solution.py:428
  23.9 19.7 %collective-permute-start = (bf16[16,18432]{1,0:T(8,128)(2,1)S(1)}, bf16[16,18432]{1,0:T(8,128)(2,1)S(1)}, u32[]{:S(2)}, u32[]{:S(2)}) collective-permute-start(bf16[16,18432]{1,0:T(8,128)(2,1)S(1)} %get-tuple-element.14._across), channel_id=1, source_target_pairs={{0,508},{4,8},{8,4},{12,16},{16,12},{20,24},{24,20},{28,32},{32,28... | collective-permute-start | bytes 1769480 | tf_op jit(solution)/shard_map/ppermute | solution.py:432
  36.9 3.9 %collective-permute-start.1 = (bf16[16,18432]{1,0:T(8,128)(2,1)S(1)}, bf16[16,18432]{1,0:T(8,128)(2,1)S(1)}, u32[]{:S(2)}, u32[]{:S(2)}) collective-permute-start(bf16[16,18432]{1,0:T(8,128)(2,1)S(1)} %get-tuple-element.18), channel_id=1, source_target_pairs={{0,4},{4,0},{8,12},{12,8},{16,20},{20,16},{24,28},{28,24},{32,36},... | collective-permute-start | bytes 1769480 | tf_op jit(solution)/shard_map/ppermute | solution.py:433
  53.4 8.2 %collective-permute-start.2 = (f32[4,128]{1,0:T(4,128)S(1)}, f32[4,128]{1,0:T(4,128)S(1)}, u32[]{:S(2)}, u32[]{:S(2)}) collective-permute-start(f32[4,128]{1,0:T(4,128)S(1)} %get-tuple-element.25), channel_id=1, source_target_pairs={{0,508},{4,8},{8,4},{12,16},{16,12},{20,24},{24,20},{28,32},{32,28... | collective-permute-start | bytes 6152 | tf_op jit(solution)/shard_map/ppermute | solution.py:440

commit v6 on v5

--- a/solution.py
+++ b/solution.py
@@ -31,55 +31,33 @@
     return pltpu.CompilerParams(vmem_limit_bytes=VMEM)
 
 
-def pack_kernel(in_ref, out_ref, tiles, sems):
-    mains = [
-        [
-            pltpu.make_async_copy(
-                in_ref.at[:, :, pl.ds(d * SEG + h * LANES, LANES)],
-                tiles.at[d, :, pl.ds(h * 128, 128), :],
-                sems.at[2 * d + h],
-            )
-            for h in range(2)
-        ]
-        for d in range(GROUPS)
-    ]
-    outs = [pltpu.make_async_copy(tiles.at[d], out_ref.at[d], sems.at[8 + d]) for d in range(GROUPS)]
-    order = range(GROUPS - 1, -1, -1)
-    for d in order:
-        for copy in mains[d]:
-            copy.start()
+def pack_kernel(in_ref, _start, _box, out_ref):
     lane = lax.broadcasted_iota(jnp.int32, (32, LANES), 1)
-    for d in order:
-        for copy in mains[d]:
-            copy.wait()
-        if d == GROUPS - 1:
-            tiles[d, :, 256:288, :] = jnp.zeros((PER, 32, LANES), BF16)
-        else:
-            for f in range(PER):
-                rows = tiles[d + 1, f, 0:128, :].astype(F32)
-                tile = rows[0:32]
+    for f in range(PER):
+        for d in range(GROUPS):
+            out_ref[d, f, 0:128, :] = in_ref[f, :, d * SEG : d * SEG + LANES]
+            out_ref[d, f, 128:256, :] = in_ref[f, :, d * SEG + LANES : d * SEG + SEG]
+            if d == GROUPS - 1:
+                out_ref[d, f, 256:288, :] = jnp.zeros((32, LANES), BF16)
+            else:
+                after = in_ref[f, :, d * SEG + SEG : d * SEG + SEG + LANES].astype(F32)
+                tile = after[0:32]
                 for i in range(1, 4):
-                    moved = pltpu.roll(rows[32 * i : 32 * i + 32], 32 * i, 1)
+                    moved = pltpu.roll(after[32 * i : 32 * i + 32], 32 * i, 1)
                     tile = jnp.where(lane < 32 * i, tile, moved)
-                tiles[d, f, 256:288, :] = tile.astype(BF16)
-        outs[d].start()
-    for copy in outs:
-        copy.wait()
-
-
-def pack(coefficients):
+                out_ref[d, f, 256:288, :] = tile.astype(BF16)
+
+
+def pack(coefficients, starts, box):
     rows = coefficients.reshape(PER, DEPTH * COMP, GROUPS * SEG)
+    whole = pl.BlockSpec(memory_space=pltpu.VMEM)
     return pl.pallas_call(
         pack_kernel,
-        in_specs=[pl.BlockSpec(memory_space=pl.ANY)],
-        out_specs=pl.BlockSpec(memory_space=pl.ANY),
+        in_specs=[whole] + [pl.BlockSpec(memory_space=pl.ANY)] * 2,
+        out_specs=whole,
         out_shape=jax.ShapeDtypeStruct((GROUPS, PER, 288, LANES), BF16),
-        scratch_shapes=[
-            pltpu.VMEM((GROUPS, PER, 288, LANES), BF16),
-            pltpu.SemaphoreType.DMA((12,)),
-        ],
-        compiler_params=pltpu.CompilerParams(vmem_limit_bytes=60 * 1024 * 1024),
-    )(rows)
+        compiler_params=params(),
+    )(rows, starts, box)
 
 
 def rows_of(frames, r):
@@ -425,8 +403,8 @@
     share = (group < GROUPS - 1).astype(jnp.int32).reshape(1)
     flag = odd.astype(jnp.int32).reshape(1)
 
-    got = lax.all_to_all(pack(coefficients), "grp", 0, 0, tiled=True)
     box = jnp.stack([starts + SZ, extents], axis=1)
+    got = lax.all_to_all(pack(coefficients, starts + SZ, box), "grp", 0, 0, tiled=True)
     across, *placed = place(flag, starts + SZ, box, got)
     chip, mid = place_near(flag, box, across, placed)
     across = lax.ppermute(across, "slab", across_chips)

time: 62.7 us -> 62.7 us (level)
  blocking collectives: 7.76 us -> 27.5 us
  waiting for transfers between devices: 12.7 us -> 3.19 us
  starting transfers between devices: 30 us -> 20.5 us
  Pallas kernels: 9.05 us -> 7.04 us
  local copies, waits for them, and re-layouts: 0.18 us -> 1.4 us
    all_to_all x0 -> x1, blocking collectives: none -> 19.7 us  [local(): lax.all_to_all(pack(coefficients, starts + SZ, box), 'grp', 0, 0, tiled=T...]
    all_to_all x1 -> x0, waiting for transfers between devices: 9.5 us -> none  [local(): got = lax.all_to_all(pack(coefficients), 'grp', 0, 0, tiled=True)]
    all_to_all x1 -> x0, starting transfers between devices: 9.41 us -> none  [local(): got = lax.all_to_all(pack(coefficients), 'grp', 0, 0, tiled=True)]
    pallas_call x1, Pallas kernels: 2.26 us -> 0.25 us  [pack(): pl.pallas_call(pack_kernel, in_specs=[whole] + [pl.BlockSpec(memory_space...]
    unnamed x0 -> x2, local copies, waits for them, and re-layouts: none -> 1.22 us
  transfers between devices with their start and end apart: 4 -> 3, of which waited for: 4 -> 3; matrix products, arithmetic and copies ran while one was open for 3% -> 2% of each run, Pallas kernels for 5% -> 5%
where the time goes in v6:
time: 62.7 us; the launch traced here: 62.3 us
  blocking collectives  27.5 us (44%)
  starting transfers between devices  20.5 us (33%)
  Pallas kernels  7.04 us (11%)
  waiting for transfers between devices  3.19 us (5%)
  other arithmetic  1.92 us (3%)
  local copies, waits for them, and re-layouts  1.4 us (2%)
  between operations  0.78 us (1%)
    all_to_all x1, blocking collectives, local(): lax.all_to_all(pack(coefficients, starts + SZ, box), 'grp', 0, 0, tiled=T...  19.7 us
    ppermute x1, starting transfers between devices, local(): across = lax.ppermute(across, 'slab', across_chips)  12 us
    all_to_all x1, blocking collectives, local(): lax.all_to_all(parts, ('slab', 'grp'), 0, 0, tiled=True, axis_index_group...  7.76 us
    ppermute x1, starting transfers between devices, local(): return finish(flag, rows, lax.ppermute(far_rows, 'slab', across_chips))  6.55 us
    pallas_call x1, Pallas kernels, near(): pl.pallas_call(near_kernel, in_specs=[pl.BlockSpec(memory_space=pltpu.SME...  2.11 us
    pallas_call x1, Pallas kernels, far(): pl.pallas_call(far_kernel, in_specs=[scalar, scalar] + [whole] * 8, out_s...  2.06 us
    ppermute x1, starting transfers between devices, local(): chip = lax.ppermute(chip, 'slab', on_chip)  1.92 us
    ppermute x1, waiting for transfers between devices, local(): return finish(flag, rows, lax.ppermute(far_rows, 'slab', across_chips))  1.65 us
  transfers between devices with their start and end apart: 3, of which 3 were waited for; matrix products, arithmetic and copies ran while one was open for 2% of the time, Pallas kernels for 5%

profile of v6, /device:TPU:2, one launch (start us, length us, event | category | flops | bytes accessed | tf_op | source)
XLA Modules:
  0.0 62.3 jit_solution(9165049675613391517)
XLA Ops:
  0.7 0.9 %subtract_add_fusion.1 = (s32[16]{0:T(128)S(1)}, s32[16]{0:T(128)S(1)}, s32[16,1]{0,1:T(1,128)S(1)}, s32[16]{0:T(128)S(1)}, s32[16]{0:T(128)S(1)}, /*index=5*/s32[16]{0:T(128)S(1)}, s32[16]{0:T(128)S(1)}) fusion(s32[2048]{0:T(1024)} %param.6, s32[]{:T(128)S(6)} %select_n.93, s32[]{:T(128)S(6)} %mul.47, s32[]{:T(128)S(6)} %mul.46, s32[2048]{0:T(1024)} %param.7, ...), kind=kLoop, calls=%fused_computation.29 | loop fusion | flops 864 | bytes 864 | tf_op jit(solution)/shard_map/add | solution.py:393
  1.6 0.1 copy.11._box.box_ref
  1.7 0.0 copy-start
  1.7 1.2 %copy-done = bf16[4,16,8,1024]{3,2,1,0:T(8,128)(2,1)S(1)} copy-done((bf16[4,16,8,1024]{3,2,1,0:T(8,128)(2,1)S(1)}, bf16[4,16,8,1024]{3,2,1,0:T(8,128)(2,1)}, u32[]{:S(2)}) %copy-start) | copy-done | bytes 1048600
  2.9 0.2 shard_map.59
  3.1 19.7 %all_to_all.10 = bf16[4,4,288,128]{3,2,1,0:T(8,128)(2,1)S(1)} all-to-all(bf16[4,4,288,128]{3,2,1,0:T(8,128)(2,1)S(1)} %shard_map.59), channel_id=1, replica_groups=mesh['slab'=128,'grp'=4] {'grp'}, dimensions={0} | all-to-all | bytes 2359296 | tf_op jit(solution)/shard_map/all_to_all | solution.py:407
  22.8 1.1 %shard_map.60 = (bf16[16,18432]{1,0:T(8,128)(2,1)S(1)}, f32[3456,128]{1,0:T(8,128)S(1)}, f32[3456,128]{1,0:T(8,128)S(1)}, f32[3456,128]{1,0:T(8,128)S(1)}) custom-call(s32[1]{0:T(128)} %bitcast.odd_ref, s32[16]{0:T(128)S(1)} %broadcast_add_fusion._start.start_ref, s32[16,2]{1,0:T(8,128)S(1)} %copy.11._box.box_ref, bf16[16,288,128]{2,1,0:T(8,128)(2,1)S(1)} %bitcast.13), custom_call_target="tpu_custom_call" | custom-call | tf_op jit(solution)/shard_map/pallas_call | solution.py:118
  24.0 12.0 %collective-permute-start = (bf16[16,18432]{1,0:T(8,128)(2,1)S(1)}, bf16[16,18432]{1,0:T(8,128)(2,1)S(1)}, u32[]{:S(2)}, u32[]{:S(2)}) collective-permute-start(bf16[16,18432]{1,0:T(8,128)(2,1)S(1)} %get-tuple-element.14._across), channel_id=1, source_target_pairs={{0,508},{4,8},{8,4},{12,16},{16,12},{20,24},{24,20},{28,32},{32,28... | collective-permute-start | bytes 1769480 | tf_op jit(solution)/shard_map/ppermute | solution.py:410
  36.0 0.8 %shard_map.61 = (bf16[16,18432]{1,0:T(8,128)(2,1)S(1)}, bf16[16,20480]{1,0:T(8,128)(2,1)S(1)}) custom-call(s32[1]{0:T(128)} %bitcast.odd_ref, s32[16,2]{1,0:T(8,128)S(1)} %copy.11._box.box_ref, bf16[16,18432]{1,0:T(8,128)(2,1)S(1)} %get-tuple-element.14._across, f32[3456,128]{1,0:T(8,128)S(1)} %get-tuple-element.15.s0, ...), custom_call_target="tpu_custom_call" | custom-call | flops 1 | bytes 1 | tf_op jit(solution)/shard_map/pallas_call | solution.py:139
  36.9 1.9 %collective-permute-start.1 = (bf16[16,18432]{1,0:T(8,128)(2,1)S(1)}, bf16[16,18432]{1,0:T(8,128)(2,1)S(1)}, u32[]{:S(2)}, u32[]{:S(2)}) collective-permute-start(bf16[16,18432]{1,0:T(8,128)(2,1)S(1)} %get-tuple-element.18), channel_id=1, source_target_pairs={{0,4},{4,0},{8,12},{12,8},{16,20},{20,16},{24,28},{28,24},{32,36},... | collective-permute-start | bytes 1769480 | tf_op jit(solution)/shard_map/ppermute | solution.py:411
  38.8 0.1 add_bitcast_fusion
  38.9 0.1 copy.13.where_ref
  39.0 0.8 %multiply_bitcast_fusion.pot_ref = f32[64,256]{1,0:T(8,128)S(1)} fusion(bf16[8,8,1024]{2,1,0:T(8,128)(2,1)} %param.4, s32[]{:T(128)S(6)} %select_n.98), kind=kLoop, calls=%fused_computation.4 | loop fusion | flops 32768 | bytes 98308 | tf_op jit(solution)/shard_map/mul | solution.py:401
  39.7 0.2 select_convert_fusion.lap_ref
  39.9 0.8 %collective-permute-done.1.chip_ref = bf16[16,18432]{1,0:T(8,128)(2,1)S(1)} collective-permute-done((bf16[16,18432]{1,0:T(8,128)(2,1)S(1)}, bf16[16,18432]{1,0:T(8,128)(2,1)S(1)}, u32[]{:S(2)}, u32[]{:S(2)}) %collective-permute-start.1) | collective-permute-done | bytes 589856 | tf_op jit(solution)/shard_map/ppermute | solution.py:411
  40.8 2.1 %shard_map.62 = (bf16[64,18432]{1,0:T(8,128)(2,1)S(1)}, bf16[32,2048]{1,0:T(8,128)(2,1)S(1)}, bf16[32,2048]{1,0:T(8,128)(2,1)S(1)}, f32[64,128]{1,0:T(8,128)S(1)}) custom-call(s32[1]{0:T(128)} %bitcast.odd_ref, s32[1]{0:T(128)} %bitcast.1.share_ref, bf16[16,18432]{1,0:T(8,128)(2,1)S(1)} %collective-permute-done.1.chip_ref, ...), custom_call_target="tpu_custom_call" | custom-call | flops 1 | bytes 1 | tf_op jit(solution)/shard_map/pallas_call | solution.py:237
  42.9 0.7 %collective-permute-done.across_ref = bf16[16,18432]{1,0:T(8,128)(2,1)S(1)} collective-permute-done((bf16[16,18432]{1,0:T(8,128)(2,1)S(1)}, bf16[16,18432]{1,0:T(8,128)(2,1)S(1)}, u32[]{:S(2)}, u32[]{:S(2)}) %collective-permute-start) | collective-permute-done | bytes 589856 | tf_op jit(solution)/shard_map/ppermute | solution.py:410
  43.6 2.1 %shard_map.63 = f32[8,8,128]{2,1,0:T(8,128)S(1)} custom-call(s32[1]{0:T(128)} %bitcast.odd_ref, s32[1]{0:T(128)} %bitcast.1.share_ref, bf16[16,18432]{1,0:T(8,128)(2,1)S(1)} %collective-permute-done.across_ref, bf16[64,18432]{1,0:T(8,128)(2,1)S(1)} %get-tuple-element.20.both_ref, bf16[32,2048]{1,0:T(8,128)(2,1)S(1)} %get-tuple-element.21.last_ref, ...), custom_call_target="tpu_custom_call" | custom-call | tf_op jit(solution)/shard_map/pallas_call | solution.py:302
  45.6 7.8 %all_to_all.11.parts_ref = f32[8,8,128]{2,1,0:T(8,128)S(1)} all-to-all(f32[8,8,128]{2,1,0:T(8,128)S(1)} %shard_map.63), channel_id=1, replica_groups={{0,1,2,3,4,5,6,7},{8,9,10,11,12,13,14,15},{16,17,18,19,20,21,22,23},{24..., dimensions={0} | all-to-all | bytes 65536 | tf_op jit(solution)/shard_map/all_to_all | solution.py:414
  53.4 6.6 %collective-permute-start.2 = (f32[4,128]{1,0:T(4,128)S(1)}, f32[4,128]{1,0:T(4,128)S(1)}, u32[]{:S(2)}, u32[]{:S(2)}) collective-permute-start(f32[4,128]{1,0:T(4,128)S(1)} %get-tuple-element.25), channel_id=1, source_target_pairs={{0,508},{4,8},{8,4},{12,16},{16,12},{20,24},{24,20},{28,32},{32,28... | collective-permute-start | bytes 6152 | tf_op jit(solution)/shard_map/ppermute | solution.py:418
  60.0 1.7 %collective-permute-done.2.far_ref = f32[4,128]{1,0:T(4,128)S(1)} collective-permute-done((f32[4,128]{1,0:T(4,128)S(1)}, f32[4,128]{1,0:T(4,128)S(1)}, u32[]{:S(2)}, u32[]{:S(2)}) %collective-permute-start.2) | collective-permute-done | bytes 2080 | tf_op jit(solution)/shard_map/ppermute | solution.py:418
  61.6 0.7 %shard_map.65 = (f32[4,80]{1,0:T(4,128)}, f32[4,80]{1,0:T(4,128)}) custom-call(s32[1]{0:T(128)} %bitcast.odd_ref, f32[16,128]{1,0:T(8,128)S(1)} %get-tuple-element.24.rows_ref, f32[4,128]{1,0:T(4,128)S(1)} %collective-permute-done.2.far_ref), custom_call_target="tpu_custom_call" | custom-call | tf_op jit(solution)/shard_map/pallas_call | solution.py:358
  (5 shorter events, 0.0 us)
Async XLA Ops:
  1.7 1.2 %copy-start = (bf16[4,16,8,1024]{3,2,1,0:T(8,128)(2,1)S(1)}, bf16[4,16,8,1024]{3,2,1,0:T(8,128)(2,1)}, u32[]{:S(2)}) copy-start(bf16[4,16,8,1024]{3,2,1,0:T(8,128)(2,1)} %param.5) | copy-start | bytes 3145732
  24.0 19.6 %collective-permute-start = (bf16[16,18432]{1,0:T(8,128)(2,1)S(1)}, bf16[16,18432]{1,0:T(8,128)(2,1)S(1)}, u32[]{:S(2)}, u32[]{:S(2)}) collective-permute-start(bf16[16,18432]{1,0:T(8,128)(2,1)S(1)} %get-tuple-element.14._across), channel_id=1, source_target_pairs={{0,508},{4,8},{8,4},{12,16},{16,12},{20,24},{24,20},{28,32},{32,28... | collective-permute-start | bytes 1769480 | tf_op jit(solution)/shard_map/ppermute | solution.py:410
  36.9 3.9 %collective-permute-start.1 = (bf16[16,18432]{1,0:T(8,128)(2,1)S(1)}, bf16[16,18432]{1,0:T(8,128)(2,1)S(1)}, u32[]{:S(2)}, u32[]{:S(2)}) collective-permute-start(bf16[16,18432]{1,0:T(8,128)(2,1)S(1)} %get-tuple-element.18), channel_id=1, source_target_pairs={{0,4},{4,0},{8,12},{12,8},{16,20},{20,16},{24,28},{28,24},{32,36},... | collective-permute-start | bytes 1769480 | tf_op jit(solution)/shard_map/ppermute | solution.py:411
  53.4 8.2 %collective-permute-start.2 = (f32[4,128]{1,0:T(4,128)S(1)}, f32[4,128]{1,0:T(4,128)S(1)}, u32[]{:S(2)}, u32[]{:S(2)}) collective-permute-start(f32[4,128]{1,0:T(4,128)S(1)} %get-tuple-element.25), channel_id=1, source_target_pairs={{0,508},{4,8},{8,4},{12,16},{16,12},{20,24},{24,20},{28,32},{32,28... | collective-permute-start | bytes 6152 | tf_op jit(solution)/shard_map/ppermute | solution.py:418
